TPU v7x, 128 devices: a whole 4x4x4 slice. The times are simulated.
128 devices in a mesh: wide: 32 (over z, y, core), narrow: 4 (over x).
Axes of the slice: x: 4, y: 4, z: 4, core: 2. Of those that a mesh axis runs over, the one named last changes fastest.
Arguments:
- face_blocks: float32 [5120, 320, 320], P(('wide', 'narrow')), may hold values from -0.3125 to 0.3125
- face_elems: int32 [5120, 2], P(('wide', 'narrow')), may hold values from 0 to 1023, as said below
- coarse_slot: int32 [1024], replicated, may hold values from 0 to 1023, as said below
- prolong: float32 [320, 135], replicated, may hold values from -0.3125 to 0.3125
- fine_residual: float32 [1024, 320], P(('wide', 'narrow')), may hold values from -6 to 6
- block_inverse: float32 [1024, 135, 135], P(('wide', 'narrow'))
Outputs:
- fine_correction: float32 [1024, 320], P(('wide', 'narrow'))
- owned_blocks: float32 [12288, 135, 135], P(('wide', 'narrow'))
Inputs may be any that keep to these rules, and one draw needn't show every extreme that they name: `coarse_slot`: A permutation: every element has its own coarse row. `face_elems`: the row and column elements of a face differ. With the owner of an element being coarse_slot // 32, among the 40 faces of each device (aligned blocks of 40 rows, devices in the order wide then narrow) at most 3 have row elements of any one owner, and for each narrow index one owner takes exactly 3 faces from every device with that narrow index.
All inputs are finite; a program needn't handle non-finite values.
Results may differ from a plain program's by a relative error of at most 0.000075.
Values sent between devices are 32-bit elements; how exact they have to be, the bound alone decides.
A program may use at most 192 MiB of HBM per device.

v0:
```python
import jax
import jax.numpy as jnp
from jax import lax
from jax.sharding import PartitionSpec as P

DAMPING = 0.7
PRECISE = lax.Precision.HIGHEST


def galerkin(blocks, prolong):
    applied = jnp.einsum("fij,jc->fic", blocks, prolong, precision=PRECISE)
    return jnp.einsum("ia,fic->fac", prolong, applied, precision=PRECISE)


def sum_into_rows(values, targets, rows_total):
    selector = (
        lax.broadcasted_iota(jnp.int32, (rows_total, targets.shape[0]), 0) == targets[None, :]
    ).astype(jnp.float32)
    return jnp.dot(selector, values, precision=PRECISE)


def local(face_blocks, face_elems, coarse_slot, prolong, fine_residual, block_inverse):
    wide_size = lax.axis_size("wide")
    narrow_size = lax.axis_size("narrow")
    dev_rows = fine_residual.shape[0]
    owner_total = dev_rows * narrow_size
    face_total = face_blocks.shape[0]
    coarse_width = prolong.shape[1]
    capacity = max(2, (2 * face_total + wide_size - 1) // wide_size)
    buffer_rows = wide_size * capacity
    coarse_rhs = jnp.dot(fine_residual, prolong, precision=PRECISE)
    sweep_one = DAMPING * jnp.einsum("snm,sm->sn", block_inverse, coarse_rhs, precision=PRECISE)
    iterate_all = lax.all_gather(sweep_one, ("wide", "narrow"), axis=0, tiled=True)
    slot_pairs = jnp.take(coarse_slot, face_elems, axis=0)
    row_slot = slot_pairs[:, 0]
    col_slot = slot_pairs[:, 1]
    target = row_slot // owner_total
    local_row = row_slot % owner_total
    selector = (target[:, None] == jnp.arange(wide_size, dtype=jnp.int32)[None, :]).astype(
        jnp.int32
    )
    ranking = jnp.sum(selector * (jnp.cumsum(selector, axis=0) - 1), axis=1)
    position = target * capacity + ranking
    coarse_blocks = galerkin(face_blocks, prolong)
    send_blocks = (
        jnp.zeros((buffer_rows, coarse_width, coarse_width), jnp.float32)
        .at[position]
        .set(coarse_blocks)
    )
    send_blocks = send_blocks.reshape(wide_size, capacity, coarse_width, coarse_width)
    labels = (
        jnp.zeros((buffer_rows, 2), jnp.int32)
        .at[position]
        .set(jnp.stack([local_row, col_slot], axis=1))
    )
    labels = labels.reshape(wide_size, capacity, 2)
    blocks = lax.all_to_all(send_blocks, "wide", split_axis=0, concat_axis=0, tiled=True)
    labels_in = lax.all_to_all(labels, "wide", split_axis=0, concat_axis=0, tiled=True)
    vectors = jnp.take(iterate_all, labels_in[..., 1], axis=0)
    results = jnp.einsum("wkac,wkc->wka", blocks, vectors, precision=PRECISE)
    targets_in = labels_in[..., 0]
    partial_sums = sum_into_rows(
        results.reshape(-1, coarse_width), targets_in.reshape(-1), owner_total
    )
    coupling = lax.psum_scatter(partial_sums, "narrow", scatter_dimension=0, tiled=True)
    update = (1.0 - DAMPING) * coarse_rhs - coupling
    sweep_two = sweep_one + DAMPING * jnp.einsum(
        "snm,sm->sn", block_inverse, update, precision=PRECISE
    )
    correction = jnp.dot(sweep_two, prolong.T, precision=PRECISE)
    return (correction, blocks.reshape(buffer_rows, coarse_width, coarse_width))


def solution(mesh):
    placed = (
        P(("wide", "narrow"), None, None),
        P(("wide", "narrow"), None),
        P(),
        P(),
        P(("wide", "narrow"), None),
        P(("wide", "narrow"), None, None),
    )
    return jax.shard_map(
        local,
        mesh=mesh,
        in_specs=placed,
        out_specs=(P(("wide", "narrow"), None), P(("wide", "narrow"), None, None)),
        check_vma=False,
    )
```

profile of v0, /device:TPU:8, one launch (start us, length us, event | category | flops | bytes accessed | tf_op | source)
XLA Modules:
  0.0 351.7 jit_solution(5267671407106277412)
XLA Ops:
  7.2 0.0 copy-start
  7.2 0.7 compare_select_fusion.1
  7.9 0.1 copy.56
  8.0 0.1 reshape.33
  8.1 0.0 copy-start.4
  8.2 1.0 gather_fusion
  9.1 0.1 reshape.32
  9.2 0.1 copy.57
  9.3 0.0 copy-done.4
  9.4 0.1 fusion.7
  9.5 0.1 reduce_window_sum.11
  9.5 0.2 select_reduce_fusion
  9.7 0.1 copy.58
  9.8 0.7 scatter_custom_fusion
  10.5 0.1 copy.59
  10.6 0.1 reshape.27
  10.7 0.6 copy.60
  11.3 8.5 %all-to-all-start = ((s32[32,3,2]{1,2,0:T(2,128)}), s32[32,3,2]{1,2,0:T(2,128)S(1)}, u32[]{:S(2)}, u32[]{:S(2)}) async-start(s32[32,3,2]{1,2,0:T(2,128)} %copy.60), calls=%async_computation | async-start | bytes 65536 | tf_op jit(solution)/shard_map/all_to_all | solution.py:58
  19.9 25.5 %fusion.1 = f32[40,320,135]{1,2,0:T(8,128)S(1)} fusion(f32[40,320,320]{2,1,0:T(8,128)} %param.6, f32[320,135]{0,1:T(8,128)S(1)} %copy-done), kind=kOutput, calls=%fused_computation.6 | convolution fusion | flops 6635520000 | bytes 23468800 | tf_op jit(solution)/shard_map/fij,jc->fic/dot_general | solution.py:11
  45.4 10.7 %convolution_bitcast_fusion = f32[40,135,135]{1,2,0:T(8,128)} fusion(f32[40,320,135]{1,2,0:T(8,128)S(1)} %fusion.1, f32[320,135]{0,1:T(8,128)S(1)} %copy-done), kind=kOutput, calls=%fused_computation.4 | convolution fusion | flops 2799360000 | bytes 10000800 | tf_op jit(solution)/shard_map/ia,fic->fac/dot_general | solution.py:12
  56.1 6.9 %copy.61 = f32[40,135,135]{2,1,0:T(8,128)} copy(f32[40,135,135]{1,2,0:T(8,128)} %convolution_bitcast_fusion) | data formatting | bytes 5832000 | tf_op jit(solution)/shard_map/ia,fic->fac/transpose | solution.py:12
  63.0 5.7 %broadcast_in_dim.31 = f32[96,135,135]{2,1,0:T(8,128)} broadcast(f32[]{:T(128)} %constant.73.clone.1), dimensions={} | broadcast | bytes 6998404 | tf_op jit(solution)/shard_map/broadcast_in_dim | solution.py:46
  68.7 12.1 %scatter_fusion = f32[96,135,135]{2,1,0:T(8,128)} fusion(f32[96,135,135]{2,1,0:T(8,128)} %broadcast_in_dim.31, s32[40]{0:T(128)S(1)} %fusion.19, f32[40,135,135]{2,1,0:T(8,128)} %copy.61), kind=kCustom, calls=%fused_computation.3 | custom fusion | bytes 8748160 | tf_op jit(solution)/shard_map/scatter | solution.py:48
  80.8 0.0 all-to-all-done
  80.8 7.6 %all-to-all-start.1 = ((f32[32,3,135,135]{3,2,1,0:T(8,128)}), f32[32,3,135,135]{3,2,1,0:T(8,128)}, u32[]{:S(2)}, u32[]{:S(2)}) async-start(f32[32,3,135,135]{3,2,1,0:T(8,128)} %bitcast.46), calls=%async_computation.1 | async-start | bytes 26738688 | tf_op jit(solution)/shard_map/all_to_all | solution.py:57
  88.4 0.0 reduce-scatter.2.cloned.1.call-start
  88.5 0.7 copy.66
  89.1 0.3 fusion.22
  89.4 0.7 fusion.15
  90.1 214.6 %all_gather.3 = f32[1024,135]{1,0:T(8,128)S(1)} all-gather(f32[8,135]{1,0:T(8,128)S(1)} %bitcast_multiply_fusion.1), channel_id=1, replica_groups=mesh['wide'=32,'narrow'=4] {'wide','narrow'}, dimensions={0}, use_global_device_ids=true | all-gather | bytes 557280 | tf_op jit(solution)/shard_map/all_gather | solution.py:33
  304.8 0.1 slice_reduce_fusion
  304.9 0.1 reshape.41
  305.0 0.7 gather_fusion.1
  305.7 0.1 compare_and_fusion
  305.8 0.1 copy.62
  305.9 0.1 copy.63
  306.0 0.1 eq.31
  306.1 0.1 select_bitcast_fusion
  306.2 0.0 all-to-all-done.1
  306.2 14.0 %fusion.3 = f32[32,3,1,135]{3,2,1,0:T(1,128)S(1)} fusion(f32[32,3,135,135]{3,2,1,0:T(8,128)} %all-to-all-done.1, f32[32,3,135,1]{2,1,0,3:T(4,128)S(1)} %select_bitcast_fusion), kind=kOutput, calls=%fused_computation.10 | convolution fusion | flops 20995200 | bytes 7102080 | tf_op jit(solution)/shard_map/wkac,wkc->wka/dot_general | solution.py:60
  320.3 0.1 reshape.29
  320.3 0.8 fusion.8
  321.1 0.0 reduce-scatter.2.cloned.1.call-update
  321.1 13.6 %copy.64 = f32[96,135,135]{0,2,1:T(8,128)} copy(f32[96,135,135]{2,1,0:T(8,128)} %bitcast.13) | data formatting | bytes 13996800
  334.7 8.0 %reduce-scatter.2.cloned.1.call-done = f32[8,135]{1,0:T(8,128)} async-done(((f32[32,135]{1,0:T(8,128)}), f32[8,135]{1,0:T(8,128)}) %reduce-scatter.2.cloned.1.call-update) | async-done | bytes 4336 | tf_op jit(solution)/shard_map/reduce_scatter | solution.py:65
  342.7 0.7 subtract_bitcast_fusion
  343.4 0.7 fusion.13
  344.0 0.8 fusion.10
  (17 shorter events, 0.2 us)
Async XLA Ops:
  7.2 12.7 %copy-start = (f32[320,135]{0,1:T(8,128)S(1)}, f32[320,135]{0,1:T(8,128)}, u32[]{:S(2)}) copy-start(f32[320,135]{0,1:T(8,128)} %param.9) | copy-start | bytes 518404
  7.2 1.0 copy-start.1
  8.1 1.2 copy-start.4
  11.3 69.5 %all-to-all-start = ((s32[32,3,2]{1,2,0:T(2,128)}), s32[32,3,2]{1,2,0:T(2,128)S(1)}, u32[]{:S(2)}, u32[]{:S(2)}) async-start(s32[32,3,2]{1,2,0:T(2,128)} %copy.60), calls=%async_computation | async-start | bytes 65536 | tf_op jit(solution)/shard_map/all_to_all | solution.py:58
  80.8 7.6 %copy-start.2 = (f32[8,135,135]{2,0,1:T(8,128)S(1)}, f32[8,135,135]{2,0,1:T(8,128)}, u32[]{:S(2)}) copy-start(f32[8,135,135]{2,0,1:T(8,128)} %param.11) | copy-start | bytes 1749604
  80.8 8.3 %copy-start.3 = (f32[8,320]{1,0:T(8,128)S(1)}, f32[8,320]{1,0:T(8,128)}, u32[]{:S(2)}) copy-start(f32[8,320]{1,0:T(8,128)} %param.10) | copy-start | bytes 30724
  80.8 225.4 %all-to-all-start.1 = ((f32[32,3,135,135]{3,2,1,0:T(8,128)}), f32[32,3,135,135]{3,2,1,0:T(8,128)}, u32[]{:S(2)}, u32[]{:S(2)}) async-start(f32[32,3,135,135]{3,2,1,0:T(8,128)} %bitcast.46), calls=%async_computation.1 | async-start | bytes 26738688 | tf_op jit(solution)/shard_map/all_to_all | solution.py:57
  88.4 254.2 %reduce-scatter.2.cloned.1.call-start = ((), (), s32[]{:S(2)}) async-start(), calls=%async_computation.3 | async-start | bytes 40960 | tf_op jit(solution)/shard_map/reduce_scatter | solution.py:65
Sparse Core Ops, SparseCore 0:
  321.2 21.3 reduce-scatter.1
where the time goes:
time: 352 us
  blocking collectives  215 us (61%)
  matrix products  53.4 us (15%)
  local copies, waits for them, and re-layouts  43.2 us (12%)
  starting transfers between devices  16.1 us (5%)
  between operations  14.3 us (4%)
  waiting for transfers between devices  7.98 us (2%)
    all_gather x1, blocking collectives, local(): lax.all_gather(sweep_one, ('wide', 'narrow'), axis=0, tiled=True)  215 us
    dot_general x1, matrix products, galerkin(): applied = jnp.einsum('fij,jc->fic', blocks, prolong, precision=PRECISE)  25.5 us
    unnamed x12, local copies, waits for them, and re-layouts  14.3 us
    dot_general x1, matrix products, local(): results = jnp.einsum('wkac,wkc->wka', blocks, vectors, precision=PRECISE)  14 us
    scatter x1, local copies, waits for them, and re-layouts, local(): send_blocks = jnp.zeros((buffer_rows, coarse_width, coarse_width), jnp.fl...  12.1 us
    dot_general x1, matrix products, galerkin(): return jnp.einsum('ia,fic->fac', prolong, applied, precision=PRECISE)  10.7 us
    all_to_all x1, starting transfers between devices, local(): lax.all_to_all(labels, 'wide', split_axis=0, concat_axis=0, tiled=True)  8.55 us
    reduce_scatter x1, waiting for transfers between devices, local(): lax.psum_scatter(partial_sums, 'narrow', scatter_dimension=0, tiled=True)  7.96 us
  transfers between devices with their start and end apart: 3, of which 1 were waited for; matrix products, arithmetic and copies ran while one was open for 22% of the time, Pallas kernels for 0%

commit v1 on v0

v1 whole, which is shorter than its diff:
```python
import functools

import jax
import jax.numpy as jnp
from jax import lax
from jax.experimental import pallas as pl
from jax.experimental.pallas import tpu as pltpu
from jax.sharding import PartitionSpec as P

DAMPING = 0.7
PRECISE = lax.Precision.HIGHEST
MESH = pl.DeviceIdType.MESH

NF = 320
NC = 135
ROWS = 136
FACES = 40
WIDE = 32
NARROW = 4
CAP = 3
SLOTS = WIDE * CAP
OWN = 32
STEP = 13


def tables_kernel(faces, slots, face_o, valid_o, col_o, row_o, count):
    def clear(i, _):
        face_o[i] = 0
        valid_o[i] = 0
        col_o[i] = 0
        row_o[i] = -1
        return 0

    def clear_count(i, _):
        count[i] = 0
        return 0

    lax.fori_loop(0, SLOTS, clear, 0)
    lax.fori_loop(0, WIDE, clear_count, 0)

    def place(f, _):
        row = slots[faces[0, f]]
        owner = row // OWN
        rank = count[owner]
        count[owner] = rank + 1
        at = owner * CAP + rank
        face_o[at] = f
        valid_o[at] = 1
        col_o[at] = slots[faces[1, f]]
        row_o[at] = row % OWN
        return 0

    lax.fori_loop(0, FACES, place, 0)


def slot_tables(face_elems, coarse_slot):
    smem = pl.BlockSpec(memory_space=pltpu.SMEM)
    return pl.pallas_call(
        tables_kernel,
        out_shape=[jax.ShapeDtypeStruct((SLOTS,), jnp.int32)] * 4,
        in_specs=[smem] * 2,
        out_specs=[smem] * 4,
        scratch_shapes=[pltpu.SMEM((WIDE,), jnp.int32)],
        name="tables",
    )(face_elems.T, coarse_slot)


def split(x):
    high = x.astype(jnp.bfloat16)
    return high, (x - high.astype(jnp.float32)).astype(jnp.bfloat16)


def dot(a, b):
    return jnp.dot(a, b, preferred_element_type=jnp.float32)


def dot_t(a, b):
    return lax.dot_general(
        a, b, (((1,), (1,)), ((), ())), precision=PRECISE, preferred_element_type=jnp.float32
    )


def jacobi(inverse, vectors):
    row = lax.broadcasted_iota(jnp.int32, (8, NC), 0)
    out = jnp.zeros((8, NC), jnp.float32)
    for s in range(8):
        out = jnp.where(row == s, dot_t(vectors, inverse[:, s, :]), out)
    return out


def exchange_kernel(
    face_t, valid_t, col_t, row_t, faces_hbm, pt, values, inverse, rhs, one,
    fine_o, main_o, rem_o,
    faces, wide_pt, p_hi, p_lo, pt_hi, pt_lo, main_s, rem_s, sums, y_s, y_r, x_s, x_r,
    face_sem, main_ss, main_rs, rem_ss, rem_rs, y_ss, y_rs, x_ss, x_rs, own_sem,
):
    w = lax.axis_index("wide")
    n = lax.axis_index("narrow")

    def load(i):
        part = pl.ds(i * 8, 8)
        return pltpu.make_async_copy(faces_hbm.at[part], faces.at[part], face_sem.at[i])

    for i in range(5):
        load(i).start()

    def partner(offset, sign):
        z, y, c = w // 8, (w // 2) % 4, w % 2
        dz, dy, dc = offset // 8, (offset // 2) % 4, offset % 2
        return ((z + sign * dz + 4) % 4) * 8 + ((y + sign * dy + 4) % 4) * 2 + (c + dc) % 2

    barrier = pltpu.get_barrier_semaphore()

    def greet(i, _):
        pl.semaphore_signal(barrier, inc=1, device_id=(partner(i, 1), n), device_id_type=MESH)
        return 0

    lax.fori_loop(1, WIDE, greet, 0)
    for i in range(1, NARROW):
        pl.semaphore_signal(barrier, inc=1, device_id=(w, (n + i) % NARROW), device_id_type=MESH)

    wide_pt[...] = jnp.zeros_like(wide_pt)
    wide_pt[0:NC, :] = pt[...]
    pt_hi[...], pt_lo[...] = split(wide_pt[0:144, :])
    p_hi[...], p_lo[...] = split(wide_pt[...].T)

    lane = lax.broadcasted_iota(jnp.int32, (ROWS, 128), 1)
    sub = lax.broadcasted_iota(jnp.int32, (ROWS, 1), 0)
    sums[...] = jnp.where(lax.broadcasted_iota(jnp.int32, (ROWS, 128), 0) == NC, -1.0, 0.0)

    def main_copy(offset, to, home):
        return pltpu.make_async_remote_copy(
            src_ref=main_s.at[pl.ds(to * CAP, CAP)],
            dst_ref=main_o.at[pl.ds(home * CAP, CAP)],
            send_sem=main_ss.at[offset], recv_sem=main_rs.at[offset],
            device_id=(to, n), device_id_type=MESH,
        )

    def rem_copy(offset, to, home):
        return pltpu.make_async_remote_copy(
            src_ref=rem_s.at[pl.ds(to * CAP, CAP)],
            dst_ref=rem_o.at[pl.ds(home * CAP, CAP)],
            send_sem=rem_ss.at[offset], recv_sem=rem_rs.at[offset],
            device_id=(to, n), device_id_type=MESH,
        )

    def y_copy(offset, to, home):
        return pltpu.make_async_remote_copy(
            src_ref=y_s.at[to], dst_ref=y_r.at[home],
            send_sem=y_ss.at[offset], recv_sem=y_rs.at[offset],
            device_id=(to, n), device_id_type=MESH,
        )

    def compute(to):
        def slot(k, _):
            s = to * CAP + k
            block = faces[face_t[s]]
            high, low = split(block)
            applied = dot(high, p_hi[...]) + dot(low, p_hi[...]) + dot(high, p_lo[...])
            high, low = split(applied)
            both = dot(pt_hi[...], high) + dot(pt_lo[...], high) + dot(pt_hi[...], low)
            both = jnp.where(valid_t[s] > 0, both[0:ROWS, :], 0.0)
            main_s[s] = both[:, 0:128]
            corner = pltpu.roll(both[128:ROWS, 128:256], 0, 1, stride=8, stride_axis=0)
            main_s[s, NC:ROWS, :] = jnp.sum(corner, axis=0, keepdims=True)
            rem_s[s] = both[0:128, 128:256].T[0:8, :]
            v = values[pl.ds(col_t[s], 1), :]
            y = jnp.sum(both[:, 0:NC] * v, axis=1, keepdims=True)
            y = jnp.where(sub == NC, row_t[s].astype(jnp.float32), y)
            sums[...] = jnp.where(lane == to * 4 + k, y, sums[...])
            return 0

        lax.fori_loop(0, CAP, slot, 0)

    for i in range(5):
        load(i).wait()
    pl.semaphore_wait(barrier, WIDE + NARROW - 2)

    def send(step, _):
        offset = ((step + 1) * STEP) % WIDE
        to = partner(offset, 1)
        compute(to)
        main_copy(offset, to, w).start()
        rem_copy(offset, to, w).start()
        return 0

    lax.fori_loop(0, WIDE - 1, send, 0)
    compute(w)
    mine = pl.ds(w * CAP, CAP)
    own_main = pltpu.make_async_copy(main_s.at[mine], main_o.at[mine], own_sem.at[0])
    own_rem = pltpu.make_async_copy(rem_s.at[mine], rem_o.at[mine], own_sem.at[1])
    own_main.start()
    own_rem.start()

    by_slot = jnp.concatenate([sums[0:128, :].T, jnp.pad(sums[128:ROWS, :].T, ((0, 0), (0, 120)))], axis=0)
    for to in range(WIDE):
        y_s[to, 0:3, :] = by_slot[4 * to : 4 * to + 3, :]
        y_s[to, 3:6, :] = by_slot[128 + 4 * to : 128 + 4 * to + 3, :]
        y_s[to, 6:8, :] = jnp.zeros((2, 128), jnp.float32)

    def send_y(offset, _):
        y_copy(offset, partner(offset, 1), w).start()
        return 0

    lax.fori_loop(1, WIDE, send_y, 0)
    y_r[w] = y_s[w]

    def wait_y(offset, _):
        y_copy(offset, partner(offset, 1), partner(offset, -1)).wait_recv()
        return 0

    lax.fori_loop(1, WIDE, wait_y, 0)

    terms = y_r[...].reshape(WIDE * 8, 128)
    labels = terms.T[7:8, :]
    place = lax.broadcasted_iota(jnp.int32, (OWN, WIDE * 8), 1) % 8
    of_row = lax.broadcasted_iota(jnp.int32, (OWN, WIDE * 8), 0).astype(jnp.float32)
    tail = jnp.where((labels == of_row) & (place >= 3) & (place < 6), 1.0, 0.0)
    head = pltpu.roll(tail, WIDE * 8 - 3, 1)
    head_sum = jnp.dot(head, terms, precision=PRECISE, preferred_element_type=jnp.float32)
    tail_sum = jnp.dot(tail, terms, precision=PRECISE, preferred_element_type=jnp.float32)
    for i in range(NARROW):
        x_s[i, 0:8, :] = head_sum[8 * i : 8 * i + 8, :]
        x_s[i, 8:16, :] = tail_sum[8 * i : 8 * i + 8, :]

    def x_copy(i, home):
        to = (n + i) % NARROW
        return pltpu.make_async_remote_copy(
            src_ref=x_s.at[to], dst_ref=x_r.at[home],
            send_sem=x_ss.at[i], recv_sem=x_rs.at[i],
            device_id=(w, to), device_id_type=MESH,
        )

    for i in range(1, NARROW):
        x_copy(i, n).start()
    x_r[n] = x_s[n]
    for i in range(1, NARROW):
        x_copy(i, (n + NARROW - i) % NARROW).wait_recv()
    total = x_r[0] + x_r[1] + x_r[2] + x_r[3]
    coupling = jnp.concatenate([total[0:8, :], total[8:16, :]], axis=1)[:, 0:NC]
    update = (1.0 - DAMPING) * rhs[...] - coupling
    two = one[...] + DAMPING * jacobi(inverse, update)
    fine_o[...] = jnp.dot(two, pt[...], precision=PRECISE, preferred_element_type=jnp.float32)

    def finish(offset, _):
        to, source = partner(offset, 1), partner(offset, -1)
        for copy in (main_copy, rem_copy):
            copy(offset, to, source).wait_recv()
        for copy in (main_copy, rem_copy, y_copy):
            copy(offset, to, w).wait_send()
        return 0

    lax.fori_loop(1, WIDE, finish, 0)
    for i in range(1, NARROW):
        x_copy(i, n).wait_send()
    own_main.wait()
    own_rem.wait()


def exchange(tables, face_blocks, pt, values, inverse, rhs, one):
    smem = pl.BlockSpec(memory_space=pltpu.SMEM)
    vmem = pl.BlockSpec(memory_space=pltpu.VMEM)
    anywhere = pl.BlockSpec(memory_space=pl.ANY)
    f32, bf16, dma = jnp.float32, jnp.bfloat16, pltpu.SemaphoreType.DMA
    return pl.pallas_call(
        exchange_kernel,
        out_shape=[
            jax.ShapeDtypeStruct((8, NF), f32),
            jax.ShapeDtypeStruct((SLOTS, ROWS, 128), f32),
            jax.ShapeDtypeStruct((SLOTS, 8, 128), f32),
        ],
        in_specs=[smem] * 4 + [anywhere] + [vmem] * 5,
        out_specs=[vmem, anywhere, anywhere],
        scratch_shapes=[
            pltpu.VMEM((FACES, NF, NF), f32),
            pltpu.VMEM((256, NF), f32),
            pltpu.VMEM((NF, 256), bf16),
            pltpu.VMEM((NF, 256), bf16),
            pltpu.VMEM((144, NF), bf16),
            pltpu.VMEM((144, NF), bf16),
            pltpu.VMEM((SLOTS, ROWS, 128), f32),
            pltpu.VMEM((SLOTS, 8, 128), f32),
            pltpu.VMEM((ROWS, 128), f32),
            pltpu.VMEM((WIDE, 8, 128), f32),
            pltpu.VMEM((WIDE, 8, 128), f32),
            pltpu.VMEM((NARROW, 16, 128), f32),
            pltpu.VMEM((NARROW, 16, 128), f32),
            dma((5,)),
        ]
        + [dma((WIDE,))] * 6
        + [dma((NARROW,))] * 2
        + [dma((2,))],
        compiler_params=pltpu.CompilerParams(
            collective_id=0, has_side_effects=True, vmem_limit_bytes=48 << 20
        ),
        cost_estimate=pl.CostEstimate(flops=10**10, bytes_accessed=35 * 10**6, transcendentals=0),
        name="exchange",
    )(*tables, face_blocks, pt, values, inverse, rhs, one)


def unpack_kernel(main, rem, out, edge):
    i = pl.program_id(0)

    @pl.when(i == 0)
    def _():
        for c in range(NC - 128):
            edge[c] = rem[:, c, :].T

    for r in range(8):
        out[r, 0:128, :] = main[:, r, :].T

    @pl.when(i < 16)
    def _():
        for c in range(NC - 128):
            out[:, 128 + c, :] = edge[c, pl.ds(pl.multiple_of(i * 8, 8), 8), :]

    @pl.when(i == 16)
    def _():
        corner = main[:, 7, :].T
        for r in range(NC - 128):
            out[r, 128:NC, :] = corner[8 * r : 8 * r + NC - 128, :]


def unpack(main, rem):
    return pl.pallas_call(
        unpack_kernel,
        grid=(17,),
        out_shape=jax.ShapeDtypeStruct((NC, NC, SLOTS), jnp.float32),
        in_specs=[
            pl.BlockSpec((SLOTS, 8, 128), lambda i: (0, i, 0)),
            pl.BlockSpec((SLOTS, 8, 128), lambda i: (0, 0, 0)),
        ],
        out_specs=pl.BlockSpec((8, NC, SLOTS), lambda i: (i, 0, 0)),
        scratch_shapes=[pltpu.VMEM((NC - 128, 128, SLOTS), jnp.float32)],
        compiler_params=pltpu.CompilerParams(vmem_limit_bytes=32 << 20),
        name="unpack",
    )(main, rem)


def local(face_blocks, face_elems, coarse_slot, prolong, fine_residual, block_inverse):
    rhs = jnp.dot(fine_residual, prolong, precision=PRECISE)
    one = DAMPING * jnp.einsum("snm,sm->sn", block_inverse, rhs, precision=PRECISE)
    values = lax.all_gather(one, ("wide", "narrow"), axis=0, tiled=True)
    tables = slot_tables(face_elems, coarse_slot)
    fine, main, rem = exchange(
        tables, face_blocks, prolong.T, values, jnp.transpose(block_inverse, (1, 0, 2)), rhs, one
    )
    return fine, jnp.transpose(unpack(main, rem), (2, 0, 1))


def solution(mesh):
    placed = (
        P(("wide", "narrow"), None, None),
        P(("wide", "narrow"), None),
        P(),
        P(),
        P(("wide", "narrow"), None),
        P(("wide", "narrow"), None, None),
    )
    return jax.shard_map(
        local,
        mesh=mesh,
        in_specs=placed,
        out_specs=(P(("wide", "narrow"), None), P(("wide", "narrow"), None, None)),
        check_vma=False,
    )
```

time: 352 us -> 198 us (0.56)
  blocking collectives: 215 us -> 60 us
  Pallas kernels: 0 us -> 128 us
  matrix products: 53.4 us -> 3.8 us
  local copies, waits for them, and re-layouts: 43.2 us -> 3.58 us
  starting transfers between devices: 16.1 us -> 0 us
  between operations: 14.3 us -> 0.74 us
  waiting for transfers between devices: 7.98 us -> 0 us
    all_gather x1, blocking collectives: 215 us -> 60 us  [local(): values = lax.all_gather(one, ('wide', 'narrow'), axis=0, tiled=True)]
    pallas_call x0 -> x3, Pallas kernels: none -> 128 us  [the longest x1 114 us: exchange(): pl.pallas_call(exchange_kernel, out_shape=[jax.ShapeDtypeStruct((8, NF),...]
    dot_general x8 -> x2, matrix products: 53.4 us -> 3.8 us  [the longest x1 2.59 us: local(): jnp.einsum('snm,sm->sn', block_inverse, rhs, precision=PRECISE)]
    all_to_all x2 -> x0, starting transfers between devices: 16.1 us -> none  [the longest x1 8.55 us: local(): lax.all_to_all(labels, 'wide', split_axis=0, concat_axis=0, tiled=True)]
    scatter x3 -> x0, local copies, waits for them, and re-layouts: 12.9 us -> none  [the longest x1 12.1 us: local(): send_blocks = jnp.zeros((buffer_rows, coarse_width, coarse_width), jnp.fl...]
    unnamed x12 -> x17, local copies, waits for them, and re-layouts: 14.3 us -> 3.58 us
    reduce_scatter x1 -> x0, waiting for transfers between devices: 7.96 us -> none  [local(): lax.psum_scatter(partial_sums, 'narrow', scatter_dimension=0, tiled=True)]
    transpose x1 -> x0, local copies, waits for them, and re-layouts: 6.91 us -> none  [galerkin(): return jnp.einsum('ia,fic->fac', prolong, applied, precision=PRECISE)]
  transfers between devices with their start and end apart: 3 -> 0, of which waited for: 1 -> 0; matrix products, arithmetic and copies ran while one was open for 22% -> 0% of each run, Pallas kernels for 0% -> 0%
where the time goes in v1:
time: 198 us; the launch traced here: 196 us
  Pallas kernels  128 us (65%)
  blocking collectives  60 us (30%)
  matrix products  3.8 us (2%)
  local copies, waits for them, and re-layouts  3.58 us (2%)
    pallas_call x1, Pallas kernels, exchange(): pl.pallas_call(exchange_kernel, out_shape=[jax.ShapeDtypeStruct((8, NF),...  114 us
    all_gather x1, blocking collectives, local(): values = lax.all_gather(one, ('wide', 'narrow'), axis=0, tiled=True)  60 us
    pallas_call x1, Pallas kernels, unpack(): pl.pallas_call(unpack_kernel, grid=(17,), out_shape=jax.ShapeDtypeStruct(...  10.5 us

profile of v1, /device:TPU:8, one launch (start us, length us, event | category | flops | bytes accessed | tf_op | source)
XLA Modules:
  0.0 196.0 jit_solution(8288393758595705821)
XLA Ops:
  0.6 0.0 copy-start
  0.6 3.3 %tables.1 = (s32[96]{0:T(128)}, s32[96]{0:T(128)}, s32[96]{0:T(128)}, s32[96]{0:T(128)}) custom-call(s32[2,40]{1,0:T(2,128)} %bitcast.13, s32[1024]{0:T(1024)} %slots.1), custom_call_target="tpu_custom_call" | custom-call | tf_op jit(solution)/shard_map/tables/pallas_call | solution.py:58
  4.0 0.0 copy-done
  4.0 1.2 fusion.3.rhs
  5.2 0.0 copy-start.2
  5.2 0.1 copy-start.3
  5.3 0.0 copy-start.4
  5.3 0.0 copy-start.5
  5.3 0.0 copy-start.6
  5.3 0.0 copy-start.7
  5.3 2.6 %fusion = f32[8,1,135]{2,1,0:T(1,128)S(1)} fusion(f32[8,135,135]{2,0,1:T(8,128)} %param.11, f32[8,135,1]{1,0,2:T(8,128)S(1)} %bitcast.11), kind=kOutput, calls=%fused_computation | convolution fusion | flops 1749600 | bytes 591840 | tf_op jit(solution)/shard_map/snm,sm->sn/dot_general | solution.py:342
  7.9 60.0 %all_gather.3.values = f32[1024,135]{1,0:T(8,128)S(1)} all-gather(f32[8,135]{1,0:T(8,128)S(1)} %bitcast_multiply_fusion.one), channel_id=1, replica_groups=mesh['wide'=32,'narrow'=4] {'wide','narrow'}, dimensions={0}, use_global_device_ids=true | all-gather | bytes 557280 | tf_op jit(solution)/shard_map/all_gather | solution.py:343
  68.0 0.0 copy-done.2
  68.0 0.0 copy-done.3
  68.0 0.0 copy-done.4
  68.0 0.0 copy-done.5
  68.0 0.0 copy-done.6
  68.0 0.0 copy-done.7
  68.0 114.0 %exchange.1 = (f32[8,320]{1,0:T(8,128)S(1)}, f32[96,136,128]{2,1,0:T(8,128)}, f32[96,8,128]{2,1,0:T(8,128)S(1)}) custom-call(s32[96]{0:T(128)S(1)} %copy-done.4, s32[96]{0:T(128)S(1)} %copy-done.5, s32[96]{0:T(128)S(1)} %copy-done.6, s32[96]{0:T(128)S(1)} %copy-done.7, f32[40,320,320]{2,1,0:T(8,128)} %faces_hbm.1, f32[135,320]{1,0:T(8,128)S(1)} %bitcast.10, ...), custom_call_target="tpu_custom_call" | custom-call | flops 10000000000 | bytes 35000000 | tf_op jit(solution)/shard_map/exchange/pallas_call | solution.py:265
  182.0 0.0 copy-start.1
  182.0 2.9 %copy-done.1 = f32[96,136,128]{2,1,0:T(8,128)S(1)} copy-done((f32[96,136,128]{2,1,0:T(8,128)S(1)}, f32[96,136,128]{2,1,0:T(8,128)}, u32[]{:S(2)}) %copy-start.1) | copy-done | bytes 6684696
  184.9 10.5 %unpack.1 = f32[135,135,96]{2,1,0:T(8,128)} custom-call(f32[96,136,128]{2,1,0:T(8,128)S(1)} %copy-done.1, f32[96,8,128]{2,1,0:T(8,128)S(1)} %get-tuple-element.15.rem), custom_call_target="tpu_custom_call" | custom-call | tf_op jit(solution)/shard_map/unpack/pallas_call | solution.py:325
  195.4 0.6 copy.17
  (1 shorter events, 0.0 us)
Async XLA Ops:
  0.6 3.4 %copy-start = (f32[8,320]{1,0:T(8,128)S(1)}, f32[8,320]{1,0:T(8,128)}, u32[]{:S(2)}) copy-start(f32[8,320]{1,0:T(8,128)} %param.10) | copy-start | bytes 30724
  5.2 62.7 %copy-start.2 = (f32[8,135,135]{2,0,1:T(8,128)S(1)}, f32[8,135,135]{2,0,1:T(8,128)}, u32[]{:S(2)}) copy-start(f32[8,135,135]{2,0,1:T(8,128)} %param.11) | copy-start | bytes 1749604
  5.2 62.7 %copy-start.3 = (f32[320,135]{0,1:T(8,128)S(1)}, f32[320,135]{0,1:T(8,128)}, u32[]{:S(2)}) copy-start(f32[320,135]{0,1:T(8,128)} %param.9) | copy-start | bytes 518404
  5.3 62.7 %copy-start.4 = (s32[96]{0:T(128)S(1)}, s32[96]{0:T(128)}, u32[]{:S(2)}) copy-start(s32[96]{0:T(128)} %get-tuple-element.9.face_t) | copy-start | bytes 1156
  5.3 62.7 %copy-start.5 = (s32[96]{0:T(128)S(1)}, s32[96]{0:T(128)}, u32[]{:S(2)}) copy-start(s32[96]{0:T(128)} %get-tuple-element.10.valid_t) | copy-start | bytes 1156
  5.3 62.7 %copy-start.6 = (s32[96]{0:T(128)S(1)}, s32[96]{0:T(128)}, u32[]{:S(2)}) copy-start(s32[96]{0:T(128)} %get-tuple-element.11.col_t) | copy-start | bytes 1156
  5.3 62.7 %copy-start.7 = (s32[96]{0:T(128)S(1)}, s32[96]{0:T(128)}, u32[]{:S(2)}) copy-start(s32[96]{0:T(128)} %get-tuple-element.12.row_t) | copy-start | bytes 1156
  182.0 2.9 %copy-start.1 = (f32[96,136,128]{2,1,0:T(8,128)S(1)}, f32[96,136,128]{2,1,0:T(8,128)}, u32[]{:S(2)}) copy-start(f32[96,136,128]{2,1,0:T(8,128)} %get-tuple-element.14.main) | copy-start | bytes 20054020

commit v2 on v1

--- a/solution.py
+++ b/solution.py
@@ -20,7 +20,29 @@
 CAP = 3
 SLOTS = WIDE * CAP
 OWN = 32
-STEP = 13
+PAIRS = (
+    (1, 1), (3, 3), (1, 3), (3, 1), (2, 1), (0, 3), (2, 3), (0, 1),
+    (1, 2), (3, 0), (3, 2), (1, 0), (2, 0), (0, 2), (2, 2),
+)
+CODES = tuple(
+    sum((4 * dz + dy) * 16**i for i, (dz, dy) in enumerate(PAIRS[at : at + 7])) for at in (0, 7, 14)
+)
+GATHER_AT, SPREAD_AT = 2, 9
+
+
+def offset_at(step):
+    i = step + 3
+    pair = i // 4 * 2 + i % 2 - 2
+    core = i // 2 % 2
+    last = step // 29
+    pair = pair * (1 - last) + 14 * last
+    core = core * (1 - last) + (step - 29) * last
+    part = pair // 7
+    first, second, third = (part - 1) * (part - 2) // 2, part * (2 - part), part * (part - 1) // 2
+    code = CODES[0] * first + CODES[1] * second + CODES[2] * third
+    offset = lax.shift_right_logical(code, 4 * (pair % 7)) % 16 * 2 + core
+    start, end = 1 - (step + 30) // 31 + step // 31, step // 31
+    return (offset * (1 - start) + start) * (1 - end)
 
 
 def tables_kernel(faces, slots, face_o, valid_o, col_o, row_o, count):
@@ -89,10 +111,12 @@
 
 
 def exchange_kernel(
-    face_t, valid_t, col_t, row_t, faces_hbm, pt, values, inverse, rhs, one,
+    face_t, valid_t, col_t, row_t, faces_hbm, pt, residual, inverse,
     fine_o, main_o, rem_o,
-    faces, wide_pt, p_hi, p_lo, pt_hi, pt_lo, main_s, rem_s, sums, y_s, y_r, x_s, x_r,
-    face_sem, main_ss, main_rs, rem_ss, rem_rs, y_ss, y_rs, x_ss, x_rs, own_sem,
+    faces, wide_pt, p_hi, p_lo, pt_hi, pt_lo, main_s, rem_s, edge_s, sums, y_s, y_r, x_s, x_r,
+    v_s, v_r, values,
+    face_sem, main_ss, main_rs, rem_ss, rem_rs, y_ss, y_rs, g_ss, g_rs, x_ss, x_rs, v_ss, v_rs,
+    core_sem, own_sem,
 ):
     w = lax.axis_index("wide")
     n = lax.axis_index("narrow")
@@ -124,6 +148,35 @@
     pt_hi[...], pt_lo[...] = split(wide_pt[0:144, :])
     p_hi[...], p_lo[...] = split(wide_pt[...].T)
 
+    rhs = dot_t(residual[...], pt[...])
+    one = DAMPING * jacobi(inverse, rhs)
+    zq, core = w // 2, w % 2
+    record = core * 16 + zq
+    v_s[0] = one[:, 0:128]
+    v_s[1] = pltpu.roll(jnp.pad(one[:, 128:NC], ((0, 0), (0, 256 - NC))), 8 * n, 1)
+
+    def v_copy(i, home):
+        return pltpu.make_async_remote_copy(
+            src_ref=v_s, dst_ref=v_r.at[home], send_sem=v_ss.at[i], recv_sem=v_rs.at[i],
+            device_id=(w, (n + i) % NARROW), device_id_type=MESH,
+        )
+
+    def g_copy(q, home):
+        chip = (zq // 4 + q // 4) % 4 * 4 + (zq % 4 + q % 4) % 4
+        return pltpu.make_async_remote_copy(
+            src_ref=values.at[record], dst_ref=values.at[core * 16 + home],
+            send_sem=g_ss.at[q], recv_sem=g_rs.at[q],
+            device_id=(chip * 2 + core, n), device_id_type=MESH,
+        )
+
+    def core_copy(half):
+        part = pl.ds(half * 16, 16)
+        return pltpu.make_async_remote_copy(
+            src_ref=values.at[part], dst_ref=values.at[part],
+            send_sem=core_sem.at[0], recv_sem=core_sem.at[1],
+            device_id=(zq * 2 + 1 - core, n), device_id_type=MESH,
+        )
+
     lane = lax.broadcasted_iota(jnp.int32, (ROWS, 128), 1)
     sub = lax.broadcasted_iota(jnp.int32, (ROWS, 1), 0)
     sums[...] = jnp.where(lax.broadcasted_iota(jnp.int32, (ROWS, 128), 0) == NC, -1.0, 0.0)
@@ -152,45 +205,88 @@
         )
 
     def compute(to):
-        def slot(k, _):
+        applied = []
+        for k in range(CAP):
+            high, low = split(faces[face_t[to * CAP + k]])
+            applied.append(dot(high, p_hi[...]) + dot(low, p_hi[...]) + dot(high, p_lo[...]))
+        for k in range(CAP):
             s = to * CAP + k
-            block = faces[face_t[s]]
-            high, low = split(block)
-            applied = dot(high, p_hi[...]) + dot(low, p_hi[...]) + dot(high, p_lo[...])
-            high, low = split(applied)
+            high, low = split(applied[k])
             both = dot(pt_hi[...], high) + dot(pt_lo[...], high) + dot(pt_hi[...], low)
             both = jnp.where(valid_t[s] > 0, both[0:ROWS, :], 0.0)
+            edge = both[:, 128:256]
             main_s[s] = both[:, 0:128]
-            corner = pltpu.roll(both[128:ROWS, 128:256], 0, 1, stride=8, stride_axis=0)
+            corner = pltpu.roll(edge[128:ROWS, :], 0, 1, stride=8, stride_axis=0)
             main_s[s, NC:ROWS, :] = jnp.sum(corner, axis=0, keepdims=True)
-            rem_s[s] = both[0:128, 128:256].T[0:8, :]
-            v = values[pl.ds(col_t[s], 1), :]
-            y = jnp.sum(both[:, 0:NC] * v, axis=1, keepdims=True)
-            y = jnp.where(sub == NC, row_t[s].astype(jnp.float32), y)
-            sums[...] = jnp.where(lane == to * 4 + k, y, sums[...])
-            return 0
-
-        lax.fori_loop(0, CAP, slot, 0)
-
+            rem_s[s] = edge[0:128, :].T[0:8, :]
+            edge_s[s] = edge
+
+    pl.semaphore_wait(barrier, WIDE + NARROW - 2)
+    for i in range(1, NARROW):
+        v_copy(i, n).start()
+    v_r[n] = v_s[...]
     for i in range(5):
         load(i).wait()
-    pl.semaphore_wait(barrier, WIDE + NARROW - 2)
 
     def send(step, _):
-        offset = ((step + 1) * STEP) % WIDE
+        offset = offset_at(step)
         to = partner(offset, 1)
         compute(to)
-        main_copy(offset, to, w).start()
-        rem_copy(offset, to, w).start()
-        return 0
-
-    lax.fori_loop(0, WIDE - 1, send, 0)
-    compute(w)
+
+        @pl.when(step < WIDE - 1)
+        def _():
+            main_copy(offset, to, w).start()
+            rem_copy(offset, to, w).start()
+
+        @pl.when(step == GATHER_AT)
+        def _():
+            for i in range(1, NARROW):
+                v_copy(i, (n + NARROW - i) % NARROW).wait_recv()
+            for i in range(NARROW):
+                values[record, i] = v_r[i, 0]
+            values[record, NARROW] = v_r[0, 1] + v_r[1, 1] + v_r[2, 1] + v_r[3, 1]
+
+            def spread(q, _):
+                g_copy(q, zq).start()
+                return 0
+
+            lax.fori_loop(1, 16, spread, 0)
+
+        @pl.when(step == SPREAD_AT)
+        def _():
+            def arrive(q, _):
+                home = (zq // 4 - q // 4 + 4) % 4 * 4 + (zq % 4 - q % 4 + 4) % 4
+                g_copy(q, home).wait_recv()
+                return 0
+
+            lax.fori_loop(1, 16, arrive, 0)
+            core_copy(core).start()
+
+        return 0
+
+    lax.fori_loop(0, WIDE, send, 0)
     mine = pl.ds(w * CAP, CAP)
     own_main = pltpu.make_async_copy(main_s.at[mine], main_o.at[mine], own_sem.at[0])
     own_rem = pltpu.make_async_copy(rem_s.at[mine], rem_o.at[mine], own_sem.at[1])
     own_main.start()
     own_rem.start()
+    core_copy(1 - core).wait_recv()
+
+    def apply(to, _):
+        for k in range(CAP):
+            s = to * CAP + k
+            device = col_t[s] // 8
+            row = pl.ds(col_t[s] % 8, 1)
+            held = device // NARROW
+            at = held % 2 * 16 + held // 2
+            head = values[at, device % NARROW, row, :]
+            tail = pltpu.roll(values[at, NARROW, row, :], (128 - 8 * (device % NARROW)) % 128, 1)
+            y = jnp.sum(main_s[s] * head + edge_s[s] * tail, axis=1, keepdims=True)
+            y = jnp.where(sub == NC, row_t[s].astype(jnp.float32), y)
+            sums[...] = jnp.where(lane == to * 4 + k, y, sums[...])
+        return 0
+
+    lax.fori_loop(0, WIDE, apply, 0)
 
     by_slot = jnp.concatenate([sums[0:128, :].T, jnp.pad(sums[128:ROWS, :].T, ((0, 0), (0, 120)))], axis=0)
     for to in range(WIDE):
@@ -238,8 +334,8 @@
         x_copy(i, (n + NARROW - i) % NARROW).wait_recv()
     total = x_r[0] + x_r[1] + x_r[2] + x_r[3]
     coupling = jnp.concatenate([total[0:8, :], total[8:16, :]], axis=1)[:, 0:NC]
-    update = (1.0 - DAMPING) * rhs[...] - coupling
-    two = one[...] + DAMPING * jacobi(inverse, update)
+    update = (1.0 - DAMPING) * rhs - coupling
+    two = one + DAMPING * jacobi(inverse, update)
     fine_o[...] = jnp.dot(two, pt[...], precision=PRECISE, preferred_element_type=jnp.float32)
 
     def finish(offset, _):
@@ -251,13 +347,21 @@
         return 0
 
     lax.fori_loop(1, WIDE, finish, 0)
+
+    def finish_spread(q, _):
+        g_copy(q, zq).wait_send()
+        return 0
+
+    lax.fori_loop(1, 16, finish_spread, 0)
+    core_copy(core).wait_send()
     for i in range(1, NARROW):
         x_copy(i, n).wait_send()
+        v_copy(i, n).wait_send()
     own_main.wait()
     own_rem.wait()
 
 
-def exchange(tables, face_blocks, pt, values, inverse, rhs, one):
+def exchange(tables, face_blocks, pt, residual, inverse):
     smem = pl.BlockSpec(memory_space=pltpu.SMEM)
     vmem = pl.BlockSpec(memory_space=pltpu.VMEM)
     anywhere = pl.BlockSpec(memory_space=pl.ANY)
@@ -269,7 +373,7 @@
             jax.ShapeDtypeStruct((SLOTS, ROWS, 128), f32),
             jax.ShapeDtypeStruct((SLOTS, 8, 128), f32),
         ],
-        in_specs=[smem] * 4 + [anywhere] + [vmem] * 5,
+        in_specs=[smem] * 4 + [anywhere] + [vmem] * 3,
         out_specs=[vmem, anywhere, anywhere],
         scratch_shapes=[
             pltpu.VMEM((FACES, NF, NF), f32),
@@ -280,22 +384,27 @@
             pltpu.VMEM((144, NF), bf16),
             pltpu.VMEM((SLOTS, ROWS, 128), f32),
             pltpu.VMEM((SLOTS, 8, 128), f32),
+            pltpu.VMEM((SLOTS, ROWS, 128), f32),
             pltpu.VMEM((ROWS, 128), f32),
             pltpu.VMEM((WIDE, 8, 128), f32),
             pltpu.VMEM((WIDE, 8, 128), f32),
             pltpu.VMEM((NARROW, 16, 128), f32),
             pltpu.VMEM((NARROW, 16, 128), f32),
+            pltpu.VMEM((2, 8, 128), f32),
+            pltpu.VMEM((NARROW, 2, 8, 128), f32),
+            pltpu.VMEM((WIDE, NARROW + 1, 8, 128), f32),
             dma((5,)),
         ]
         + [dma((WIDE,))] * 6
-        + [dma((NARROW,))] * 2
-        + [dma((2,))],
+        + [dma((16,))] * 2
+        + [dma((NARROW,))] * 4
+        + [dma((2,))] * 2,
         compiler_params=pltpu.CompilerParams(
-            collective_id=0, has_side_effects=True, vmem_limit_bytes=48 << 20
+            collective_id=0, has_side_effects=True, vmem_limit_bytes=52 << 20
         ),
         cost_estimate=pl.CostEstimate(flops=10**10, bytes_accessed=35 * 10**6, transcendentals=0),
         name="exchange",
-    )(*tables, face_blocks, pt, values, inverse, rhs, one)
+    )(*tables, face_blocks, pt, residual, inverse)
 
 
 def unpack_kernel(main, rem, out, edge):
@@ -338,12 +447,9 @@
 
 
 def local(face_blocks, face_elems, coarse_slot, prolong, fine_residual, block_inverse):
-    rhs = jnp.dot(fine_residual, prolong, precision=PRECISE)
-    one = DAMPING * jnp.einsum("snm,sm->sn", block_inverse, rhs, precision=PRECISE)
-    values = lax.all_gather(one, ("wide", "narrow"), axis=0, tiled=True)
     tables = slot_tables(face_elems, coarse_slot)
     fine, main, rem = exchange(
-        tables, face_blocks, prolong.T, values, jnp.transpose(block_inverse, (1, 0, 2)), rhs, one
+        tables, face_blocks, prolong.T, fine_residual, jnp.transpose(block_inverse, (1, 0, 2))
     )
     return fine, jnp.transpose(unpack(main, rem), (2, 0, 1))
 

time: 198 us -> 134 us (0.68); the launches traced: 196 us -> 134 us
  blocking collectives: 60 us -> 0 us
  local copies, waits for them, and re-layouts: 3.58 us -> 8.95 us
  Pallas kernels: 128 us -> 124 us
  matrix products: 3.8 us -> 0 us
    all_gather x1 -> x0, blocking collectives: 60 us -> none  [local(): values = lax.all_gather(one, ('wide', 'narrow'), axis=0, tiled=True)]
    unnamed x17, local copies, waits for them, and re-layouts: 3.58 us -> 8.95 us
    dot_general x2 -> x0, matrix products: 3.8 us -> none  [the longest x1 2.59 us: local(): jnp.einsum('snm,sm->sn', block_inverse, rhs, precision=PRECISE)]
    pallas_call x1, Pallas kernels: 114 us -> 111 us  [exchange(): pl.pallas_call(exchange_kernel, out_shape=[jax.ShapeDtypeStruct((8, NF),...]
where the time goes in v2:
time: 134 us
  Pallas kernels  124 us (93%)
  local copies, waits for them, and re-layouts  8.95 us (7%)
    pallas_call x1, Pallas kernels, exchange(): pl.pallas_call(exchange_kernel, out_shape=[jax.ShapeDtypeStruct((8, NF),...  111 us
    pallas_call x1, Pallas kernels, unpack(): pl.pallas_call(unpack_kernel, grid=(17,), out_shape=jax.ShapeDtypeStruct(...  10.5 us
    unnamed x17, local copies, waits for them, and re-layouts  8.95 us
    pallas_call x1, Pallas kernels, slot_tables(): pl.pallas_call(tables_kernel, out_shape=[jax.ShapeDtypeStruct((SLOTS,), j...  3.2 us

profile of v2, /device:TPU:8, one launch (start us, length us, event | category | flops | bytes accessed | tf_op | source)
XLA Modules:
  0.0 134.0 jit_solution(4188158927340905961)
XLA Ops:
  0.6 3.2 %tables.1 = (s32[96]{0:T(128)}, s32[96]{0:T(128)}, s32[96]{0:T(128)}, s32[96]{0:T(128)}) custom-call(s32[2,40]{1,0:T(2,128)} %bitcast.7, s32[1024]{0:T(1024)} %slots.1), custom_call_target="tpu_custom_call" | custom-call | tf_op jit(solution)/shard_map/tables/pallas_call | solution.py:80
  3.8 0.0 copy-start.1
  3.9 1.2 copy-done.1
  5.1 0.0 copy-start.2
  5.1 0.9 copy-done.2
  6.0 0.0 copy-start.3
  6.0 0.7 copy-done.3
  6.7 0.0 copy-start.4
  6.7 0.7 copy-done.4
  7.4 0.0 copy-start.5
  7.4 0.7 copy-done.5
  8.0 0.0 copy-start.6
  8.0 0.7 copy-done.6
  8.7 0.0 copy-start.7
  8.7 0.6 copy-done.7
  9.3 110.7 %exchange.1 = (f32[8,320]{1,0:T(8,128)S(1)}, f32[96,136,128]{2,1,0:T(8,128)}, f32[96,8,128]{2,1,0:T(8,128)S(1)}) custom-call(s32[96]{0:T(128)S(1)} %copy-done.4, s32[96]{0:T(128)S(1)} %copy-done.5, s32[96]{0:T(128)S(1)} %copy-done.6, s32[96]{0:T(128)S(1)} %copy-done.7, f32[40,320,320]{2,1,0:T(8,128)} %faces_hbm.1, f32[135,320]{1,0:T(8,128)S(1)} %bitcast.5, ...), custom_call_target="tpu_custom_call" | custom-call | flops 10000000000 | bytes 35000000 | tf_op jit(solution)/shard_map/exchange/pallas_call | solution.py:369
  120.0 0.0 copy-start
  120.0 2.9 %copy-done = f32[96,136,128]{2,1,0:T(8,128)S(1)} copy-done((f32[96,136,128]{2,1,0:T(8,128)S(1)}, f32[96,136,128]{2,1,0:T(8,128)}, u32[]{:S(2)}) %copy-start) | copy-done | bytes 6684696
  122.9 10.5 %unpack.1 = f32[135,135,96]{2,1,0:T(8,128)} custom-call(f32[96,136,128]{2,1,0:T(8,128)S(1)} %copy-done, f32[96,8,128]{2,1,0:T(8,128)S(1)} %get-tuple-element.15.rem), custom_call_target="tpu_custom_call" | custom-call | tf_op jit(solution)/shard_map/unpack/pallas_call | solution.py:434
  133.4 0.6 copy.9
Async XLA Ops:
  3.8 1.2 copy-start.1
  5.1 0.9 copy-start.2
  6.0 0.7 copy-start.3
  6.7 0.7 copy-start.4
  7.4 0.7 copy-start.5
  8.0 0.7 copy-start.6
  8.7 0.6 copy-start.7
  120.0 2.9 %copy-start = (f32[96,136,128]{2,1,0:T(8,128)S(1)}, f32[96,136,128]{2,1,0:T(8,128)}, u32[]{:S(2)}) copy-start(f32[96,136,128]{2,1,0:T(8,128)} %get-tuple-element.14.main) | copy-start | bytes 20054020

commit v3 on v2

--- a/solution.py
+++ b/solution.py
@@ -14,6 +14,7 @@
 NF = 320
 NC = 135
 ROWS = 136
+PART = 45
 FACES = 40
 WIDE = 32
 NARROW = 4
@@ -28,63 +29,57 @@
     sum((4 * dz + dy) * 16**i for i, (dz, dy) in enumerate(PAIRS[at : at + 7])) for at in (0, 7, 14)
 )
 GATHER_AT, SPREAD_AT = 2, 9
+HELD = 26
 
 
 def offset_at(step):
-    i = step + 3
-    pair = i // 4 * 2 + i % 2 - 2
-    core = i // 2 % 2
-    last = step // 29
-    pair = pair * (1 - last) + 14 * last
-    core = core * (1 - last) + (step - 29) * last
+    last, near = step // 28, step // 30
+    pair = (step // 4 * 2 + step % 2) * (1 - last) + 14 * last
+    core = step // 2 % 2 * (1 - last) + (step - 28) * last
     part = pair // 7
     first, second, third = (part - 1) * (part - 2) // 2, part * (2 - part), part * (part - 1) // 2
     code = CODES[0] * first + CODES[1] * second + CODES[2] * third
     offset = lax.shift_right_logical(code, 4 * (pair % 7)) % 16 * 2 + core
-    start, end = 1 - (step + 30) // 31 + step // 31, step // 31
-    return (offset * (1 - start) + start) * (1 - end)
-
-
-def tables_kernel(faces, slots, face_o, valid_o, col_o, row_o, count):
+    return offset * (1 - near) + (31 - step) * near
+
+
+def tables_kernel(faces, slots, word_o, count):
     def clear(i, _):
-        face_o[i] = 0
-        valid_o[i] = 0
-        col_o[i] = 0
-        row_o[i] = -1
+        word_o[i] = 0
         return 0
 
     def clear_count(i, _):
         count[i] = 0
         return 0
 
-    lax.fori_loop(0, SLOTS, clear, 0)
-    lax.fori_loop(0, WIDE, clear_count, 0)
+    lax.fori_loop(0, 128, clear, 0, unroll=8)
+    lax.fori_loop(0, WIDE, clear_count, 0, unroll=8)
 
     def place(f, _):
         row = slots[faces[0, f]]
-        owner = row // OWN
+        owner = lax.shift_right_logical(row, 5)
         rank = count[owner]
         count[owner] = rank + 1
-        at = owner * CAP + rank
-        face_o[at] = f
-        valid_o[at] = 1
-        col_o[at] = slots[faces[1, f]]
-        row_o[at] = row % OWN
-        return 0
-
-    lax.fori_loop(0, FACES, place, 0)
-
-
-def slot_tables(face_elems, coarse_slot):
+        word_o[owner * CAP + rank] = (1 << 21) + (row & (OWN - 1)) * 65536 + slots[faces[1, f]] * 64 + f
+        return 0
+
+    lax.fori_loop(0, FACES, place, 0, unroll=4)
+
+
+def slot_table(face_elems, coarse_slot):
     smem = pl.BlockSpec(memory_space=pltpu.SMEM)
     return pl.pallas_call(
         tables_kernel,
-        out_shape=[jax.ShapeDtypeStruct((SLOTS,), jnp.int32)] * 4,
+        out_shape=jax.ShapeDtypeStruct((128,), jnp.int32),
         in_specs=[smem] * 2,
-        out_specs=[smem] * 4,
+        out_specs=smem,
         scratch_shapes=[pltpu.SMEM((WIDE,), jnp.int32)],
         name="tables",
     )(face_elems.T, coarse_slot)
+
+
+def shifted(word, by, bits):
+    return lax.shift_right_logical(word, by) & ((1 << bits) - 1)
 
 
 def split(x):
@@ -111,11 +106,11 @@
 
 
 def exchange_kernel(
-    face_t, valid_t, col_t, row_t, faces_hbm, pt, residual, inverse,
+    word_hbm, faces_hbm, pt_hbm, residual_hbm, inverse_hbm,
     fine_o, main_o, rem_o,
-    faces, wide_pt, p_hi, p_lo, pt_hi, pt_lo, main_s, rem_s, edge_s, sums, y_s, y_r, x_s, x_r,
+    word, pt, residual, inverse, faces, wide_pt, p_hi, p_lo, pt_hi, pt_lo, main_s, rem_s, edge_s, sums, y_s, y_r, x_s, x_r,
     v_s, v_r, values,
-    face_sem, main_ss, main_rs, rem_ss, rem_rs, y_ss, y_rs, g_ss, g_rs, x_ss, x_rs, v_ss, v_rs,
+    in_sem, face_sem, main_ss, main_rs, rem_ss, rem_rs, y_ss, y_rs, g_ss, g_rs, x_ss, x_rs, v_ss, v_rs,
     core_sem, own_sem,
 ):
     w = lax.axis_index("wide")
@@ -125,6 +120,14 @@
         part = pl.ds(i * 8, 8)
         return pltpu.make_async_copy(faces_hbm.at[part], faces.at[part], face_sem.at[i])
 
+    inputs = [
+        pltpu.make_async_copy(source, target, in_sem.at[i])
+        for i, (source, target) in enumerate(
+            ((pt_hbm, pt), (residual_hbm, residual), (inverse_hbm, inverse), (word_hbm, word))
+        )
+    ]
+    for copy in inputs:
+        copy.start()
     for i in range(5):
         load(i).start()
 
@@ -143,6 +146,8 @@
     for i in range(1, NARROW):
         pl.semaphore_signal(barrier, inc=1, device_id=(w, (n + i) % NARROW), device_id_type=MESH)
 
+    for copy in inputs:
+        copy.wait()
     wide_pt[...] = jnp.zeros_like(wide_pt)
     wide_pt[0:NC, :] = pt[...]
     pt_hi[...], pt_lo[...] = split(wide_pt[0:144, :])
@@ -207,13 +212,13 @@
     def compute(to):
         applied = []
         for k in range(CAP):
-            high, low = split(faces[face_t[to * CAP + k]])
+            high, low = split(faces[shifted(word[to * CAP + k], 0, 6)])
             applied.append(dot(high, p_hi[...]) + dot(low, p_hi[...]) + dot(high, p_lo[...]))
         for k in range(CAP):
             s = to * CAP + k
             high, low = split(applied[k])
             both = dot(pt_hi[...], high) + dot(pt_lo[...], high) + dot(pt_hi[...], low)
-            both = jnp.where(valid_t[s] > 0, both[0:ROWS, :], 0.0)
+            both = jnp.where(shifted(word[s], 21, 1) > 0, both[0:ROWS, :], 0.0)
             edge = both[:, 128:256]
             main_s[s] = both[:, 0:128]
             corner = pltpu.roll(edge[128:ROWS, :], 0, 1, stride=8, stride_axis=0)
@@ -233,7 +238,7 @@
         to = partner(offset, 1)
         compute(to)
 
-        @pl.when(step < WIDE - 1)
+        @pl.when((step < HELD) | (step == WIDE - 2))
         def _():
             main_copy(offset, to, w).start()
             rem_copy(offset, to, w).start()
@@ -275,14 +280,14 @@
     def apply(to, _):
         for k in range(CAP):
             s = to * CAP + k
-            device = col_t[s] // 8
-            row = pl.ds(col_t[s] % 8, 1)
-            held = device // NARROW
-            at = held % 2 * 16 + held // 2
-            head = values[at, device % NARROW, row, :]
-            tail = pltpu.roll(values[at, NARROW, row, :], (128 - 8 * (device % NARROW)) % 128, 1)
+            row = pl.ds(shifted(word[s], 6, 3), 1)
+            narrow = shifted(word[s], 9, 2)
+            at = shifted(word[s], 11, 1) * 16 + shifted(word[s], 12, 4)
+            head = values[at, narrow, row, :]
+            tail = pltpu.roll(values[at, NARROW, row, :], (128 - 8 * narrow) % 128, 1)
             y = jnp.sum(main_s[s] * head + edge_s[s] * tail, axis=1, keepdims=True)
-            y = jnp.where(sub == NC, row_t[s].astype(jnp.float32), y)
+            label = shifted(word[s], 16, 5) * shifted(word[s], 21, 1) - 1 + shifted(word[s], 21, 1)
+            y = jnp.where(sub == NC, label.astype(jnp.float32), y)
             sums[...] = jnp.where(lane == to * 4 + k, y, sums[...])
         return 0
 
@@ -300,6 +305,15 @@
 
     lax.fori_loop(1, WIDE, send_y, 0)
     y_r[w] = y_s[w]
+
+    def send_held(step, _):
+        offset = offset_at(step)
+        to = partner(offset, 1)
+        main_copy(offset, to, w).start()
+        rem_copy(offset, to, w).start()
+        return 0
+
+    lax.fori_loop(HELD, WIDE - 2, send_held, 0)
 
     def wait_y(offset, _):
         y_copy(offset, partner(offset, 1), partner(offset, -1)).wait_recv()
@@ -361,8 +375,8 @@
     own_rem.wait()
 
 
-def exchange(tables, face_blocks, pt, residual, inverse):
-    smem = pl.BlockSpec(memory_space=pltpu.SMEM)
+def exchange(table, face_blocks, pt, residual, inverse):
+    hbm = pl.BlockSpec(memory_space=pltpu.HBM)
     vmem = pl.BlockSpec(memory_space=pltpu.VMEM)
     anywhere = pl.BlockSpec(memory_space=pl.ANY)
     f32, bf16, dma = jnp.float32, jnp.bfloat16, pltpu.SemaphoreType.DMA
@@ -373,9 +387,13 @@
             jax.ShapeDtypeStruct((SLOTS, ROWS, 128), f32),
             jax.ShapeDtypeStruct((SLOTS, 8, 128), f32),
         ],
-        in_specs=[smem] * 4 + [anywhere] + [vmem] * 3,
+        in_specs=[hbm] * 5,
         out_specs=[vmem, anywhere, anywhere],
         scratch_shapes=[
+            pltpu.SMEM((128,), jnp.int32),
+            pltpu.VMEM((NC, NF), f32),
+            pltpu.VMEM((8, NF), f32),
+            pltpu.VMEM((NC, 8, NC), f32),
             pltpu.VMEM((FACES, NF, NF), f32),
             pltpu.VMEM((256, NF), f32),
             pltpu.VMEM((NF, 256), bf16),
@@ -393,6 +411,7 @@
             pltpu.VMEM((2, 8, 128), f32),
             pltpu.VMEM((NARROW, 2, 8, 128), f32),
             pltpu.VMEM((WIDE, NARROW + 1, 8, 128), f32),
+            dma((4,)),
             dma((5,)),
         ]
         + [dma((WIDE,))] * 6
@@ -400,58 +419,68 @@
         + [dma((NARROW,))] * 4
         + [dma((2,))] * 2,
         compiler_params=pltpu.CompilerParams(
-            collective_id=0, has_side_effects=True, vmem_limit_bytes=52 << 20
+            collective_id=0, has_side_effects=True, vmem_limit_bytes=42 << 20
         ),
         cost_estimate=pl.CostEstimate(flops=10**10, bytes_accessed=35 * 10**6, transcendentals=0),
         name="exchange",
-    )(*tables, face_blocks, pt, residual, inverse)
-
-
-def unpack_kernel(main, rem, out, edge):
+    )(table, face_blocks, pt, residual, inverse)
+
+
+def unpack_kernel(main, rem, fine_in, out, fine, edge):
     i = pl.program_id(0)
+    rest = NC - 128
+
+    def row(a):
+        return main[pl.ds(a, SLOTS, stride=ROWS), :].T
 
     @pl.when(i == 0)
     def _():
-        for c in range(NC - 128):
-            edge[c] = rem[:, c, :].T
-
-    for r in range(8):
-        out[r, 0:128, :] = main[:, r, :].T
-
-    @pl.when(i < 16)
-    def _():
-        for c in range(NC - 128):
-            out[:, 128 + c, :] = edge[c, pl.ds(pl.multiple_of(i * 8, 8), 8), :]
-
-    @pl.when(i == 16)
-    def _():
-        corner = main[:, 7, :].T
-        for r in range(NC - 128):
-            out[r, 128:NC, :] = corner[8 * r : 8 * r + NC - 128, :]
-
-
-def unpack(main, rem):
+        fine[...] = fine_in[...]
+        for c in range(rest):
+            edge[c] = rem[pl.ds(c, SLOTS, stride=8), :].T
+
+    for j in range(NC // PART):
+
+        @pl.when(i == j)
+        def _(j=j):
+            for r in range(PART):
+                out[r, 0:128, :] = row(j * PART + r)
+            size = min(PART, 128 - j * PART)
+            for c in range(rest):
+                out[0:size, 128 + c, :] = edge[c, j * PART : j * PART + size, :]
+            if size < PART:
+                corner = row(NC)
+                for r in range(rest):
+                    out[size + r, 128:NC, :] = corner[8 * r : 8 * r + rest, :]
+
+
+def unpack(main, rem, fine):
+    vmem = pl.BlockSpec(memory_space=pltpu.VMEM)
     return pl.pallas_call(
         unpack_kernel,
-        grid=(17,),
-        out_shape=jax.ShapeDtypeStruct((NC, NC, SLOTS), jnp.float32),
-        in_specs=[
-            pl.BlockSpec((SLOTS, 8, 128), lambda i: (0, i, 0)),
-            pl.BlockSpec((SLOTS, 8, 128), lambda i: (0, 0, 0)),
+        grid=(NC // PART,),
+        out_shape=[
+            jax.ShapeDtypeStruct((NC, NC, SLOTS), jnp.float32),
+            jax.ShapeDtypeStruct((8, NF), jnp.float32),
         ],
-        out_specs=pl.BlockSpec((8, NC, SLOTS), lambda i: (i, 0, 0)),
+        in_specs=[vmem] * 3,
+        out_specs=[
+            pl.BlockSpec((PART, NC, SLOTS), lambda i: (i, 0, 0)),
+            pl.BlockSpec((8, NF), lambda i: (0, 0)),
+        ],
         scratch_shapes=[pltpu.VMEM((NC - 128, 128, SLOTS), jnp.float32)],
-        compiler_params=pltpu.CompilerParams(vmem_limit_bytes=32 << 20),
+        compiler_params=pltpu.CompilerParams(vmem_limit_bytes=40 << 20),
         name="unpack",
-    )(main, rem)
+    )(main, rem, fine)
 
 
 def local(face_blocks, face_elems, coarse_slot, prolong, fine_residual, block_inverse):
-    tables = slot_tables(face_elems, coarse_slot)
+    table = slot_table(face_elems, coarse_slot)
     fine, main, rem = exchange(
-        tables, face_blocks, prolong.T, fine_residual, jnp.transpose(block_inverse, (1, 0, 2))
+        table, face_blocks, prolong.T, fine_residual, jnp.transpose(block_inverse, (1, 0, 2))
     )
-    return fine, jnp.transpose(unpack(main, rem), (2, 0, 1))
+    owned, fine = unpack(main.reshape(SLOTS * ROWS, 128), rem.reshape(SLOTS * 8, 128), fine)
+    return fine, jnp.transpose(owned, (2, 0, 1))
 
 
 def solution(mesh):

time: 134 us -> 118 us (0.88)
  the two profiles are of different devices: /device:TPU:8 before, /device:TPU:16 now
where the time goes in v3:
time: 118 us
  Pallas kernels  114 us (97%)
  local copies, waits for them, and re-layouts  3.53 us (3%)
    pallas_call x1, Pallas kernels, exchange(): pl.pallas_call(exchange_kernel, out_shape=[jax.ShapeDtypeStruct((8, NF),...  107 us
    pallas_call x1, Pallas kernels, unpack(): pl.pallas_call(unpack_kernel, grid=(NC // PART,), out_shape=[jax.ShapeDty...  5.21 us
    unnamed x8, local copies, waits for them, and re-layouts  3.53 us

profile of v3, /device:TPU:16, one launch (start us, length us, event | category | flops | bytes accessed | tf_op | source)
XLA Modules:
  0.0 118.2 jit_solution(14817017155425704011)
XLA Ops:
  0.6 1.7 %tables.1.word_hbm = s32[128]{0:T(128)} custom-call(s32[2,40]{1,0:T(2,128)} %bitcast.10, s32[1024]{0:T(1024)} %slots.1), custom_call_target="tpu_custom_call" | custom-call | tf_op jit(solution)/shard_map/tables/pallas_call | solution.py:71
  2.4 0.0 copy-start
  2.4 0.6 copy-done
  3.0 0.0 copy-start.1
  3.0 1.2 %copy-done.1 = f32[8,135,135]{2,0,1:T(8,128)S(1)} copy-done((f32[8,135,135]{2,0,1:T(8,128)S(1)}, f32[8,135,135]{2,0,1:T(8,128)}, u32[]{:S(2)}) %copy-start.1) | copy-done | bytes 583224
  4.3 0.0 copy-start.2
  4.3 0.9 copy-done.2
  5.2 0.0 copy-start.3
  5.2 0.7 copy-done.3
  5.9 107.0 %exchange.1 = (f32[8,320]{1,0:T(8,128)S(1)}, f32[96,136,128]{2,1,0:T(8,128)S(1)}, f32[96,8,128]{2,1,0:T(8,128)S(1)}) custom-call(s32[128]{0:T(128)S(1)} %copy-done, f32[40,320,320]{2,1,0:T(8,128)} %faces_hbm.1, f32[135,320]{1,0:T(8,128)S(1)} %bitcast.9, f32[8,320]{1,0:T(8,128)S(1)} %copy-done.3, f32[135,8,135]{2,1,0:T(8,128)S(1)} %bitcast.8), custom_call_target="tpu_custom_call" | custom-call | flops 10000000000 | bytes 35000000 | tf_op jit(solution)/shard_map/exchange/pallas_call | solution.py:383
  113.0 5.2 %unpack.1 = (f32[135,135,96]{2,1,0:T(8,128)}, f32[8,320]{1,0:T(8,128)}) custom-call(f32[13056,128]{1,0:T(8,128)S(1)} %bitcast.6, f32[768,128]{1,0:T(8,128)S(1)} %bitcast.7, f32[8,320]{1,0:T(8,128)S(1)} %get-tuple-element.9.fine_in), custom_call_target="tpu_custom_call" | custom-call | tf_op jit(solution)/shard_map/unpack/pallas_call | solution.py:459
Async XLA Ops:
  2.4 0.7 copy-start
  3.0 1.2 %copy-start.1 = (f32[8,135,135]{2,0,1:T(8,128)S(1)}, f32[8,135,135]{2,0,1:T(8,128)}, u32[]{:S(2)}) copy-start(f32[8,135,135]{2,0,1:T(8,128)} %param.11) | copy-start | bytes 1749604
  4.3 0.9 copy-start.2
  5.2 0.7 copy-start.3

commit v4 on v3

--- a/solution.py
+++ b/solution.py
@@ -28,7 +28,7 @@
 CODES = tuple(
     sum((4 * dz + dy) * 16**i for i, (dz, dy) in enumerate(PAIRS[at : at + 7])) for at in (0, 7, 14)
 )
-GATHER_AT, SPREAD_AT = 2, 9
+CORE_AT, NARROW_AT = 2, 5
 HELD = 26
 
 
@@ -43,39 +43,21 @@
     return offset * (1 - near) + (31 - step) * near
 
 
-def tables_kernel(faces, slots, word_o, count):
-    def clear(i, _):
-        word_o[i] = 0
-        return 0
-
-    def clear_count(i, _):
-        count[i] = 0
-        return 0
-
-    lax.fori_loop(0, 128, clear, 0, unroll=8)
-    lax.fori_loop(0, WIDE, clear_count, 0, unroll=8)
-
-    def place(f, _):
+def slot_words(faces, slots):
+    lane = lax.broadcasted_iota(jnp.int32, (1, 128), 1)
+
+    def place(f, words):
+        first, second, third = words
         row = slots[faces[0, f]]
-        owner = lax.shift_right_logical(row, 5)
-        rank = count[owner]
-        count[owner] = rank + 1
-        word_o[owner * CAP + rank] = (1 << 21) + (row & (OWN - 1)) * 65536 + slots[faces[1, f]] * 64 + f
-        return 0
-
-    lax.fori_loop(0, FACES, place, 0, unroll=4)
-
-
-def slot_table(face_elems, coarse_slot):
-    smem = pl.BlockSpec(memory_space=pltpu.SMEM)
-    return pl.pallas_call(
-        tables_kernel,
-        out_shape=jax.ShapeDtypeStruct((128,), jnp.int32),
-        in_specs=[smem] * 2,
-        out_specs=smem,
-        scratch_shapes=[pltpu.SMEM((WIDE,), jnp.int32)],
-        name="tables",
-    )(face_elems.T, coarse_slot)
+        word = (1 << 21) + (row & (OWN - 1)) * 65536 + slots[faces[1, f]] * 64 + f
+        here = lane == lax.shift_right_logical(row, 5)
+        third = jnp.where(here & (second > 0), word, third)
+        second = jnp.where(here & (first > 0) & (second == 0), word, second)
+        first = jnp.where(here & (first == 0), word, first)
+        return first, second, third
+
+    empty = jnp.zeros((1, 128), jnp.int32)
+    return lax.fori_loop(0, FACES, place, (empty, empty, empty), unroll=4)
 
 
 def shifted(word, by, bits):
@@ -106,11 +88,11 @@
 
 
 def exchange_kernel(
-    word_hbm, faces_hbm, pt_hbm, residual_hbm, inverse_hbm,
+    elems_hbm, slots_hbm, faces_hbm, pt_hbm, residual_hbm, inverse_hbm,
     fine_o, main_o, rem_o,
-    word, pt, residual, inverse, faces, wide_pt, p_hi, p_lo, pt_hi, pt_lo, main_s, rem_s, edge_s, sums, y_s, y_r, x_s, x_r,
-    v_s, v_r, values,
-    in_sem, face_sem, main_ss, main_rs, rem_ss, rem_rs, y_ss, y_rs, g_ss, g_rs, x_ss, x_rs, v_ss, v_rs,
+    elems, slots, words, word, pt, residual, inverse, faces, wide_pt, p_hi, p_lo, pt_hi, pt_lo, main_s, rem_s, edge_s, sums, y_s, y_r, x_s, x_r,
+    values,
+    in_sem, word_sem, face_sem, main_ss, main_rs, rem_ss, rem_rs, y_ss, y_rs, g_ss, g_rs, x_ss, x_rs, v_ss, v_rs,
     core_sem, own_sem,
 ):
     w = lax.axis_index("wide")
@@ -123,7 +105,7 @@
     inputs = [
         pltpu.make_async_copy(source, target, in_sem.at[i])
         for i, (source, target) in enumerate(
-            ((pt_hbm, pt), (residual_hbm, residual), (inverse_hbm, inverse), (word_hbm, word))
+            ((elems_hbm, elems), (slots_hbm, slots), (pt_hbm, pt), (residual_hbm, residual), (inverse_hbm, inverse))
         )
     ]
     for copy in inputs:
@@ -156,20 +138,19 @@
     rhs = dot_t(residual[...], pt[...])
     one = DAMPING * jacobi(inverse, rhs)
     zq, core = w // 2, w % 2
-    record = core * 16 + zq
-    v_s[0] = one[:, 0:128]
-    v_s[1] = pltpu.roll(jnp.pad(one[:, 128:NC], ((0, 0), (0, 256 - NC))), 8 * n, 1)
+    values[n, core * 16 + zq, 0] = one[:, 0:128]
+    values[n, core * 16 + zq, 1] = jnp.pad(one[:, 128:NC], ((0, 0), (0, 256 - NC)))
 
     def v_copy(i, home):
         return pltpu.make_async_remote_copy(
-            src_ref=v_s, dst_ref=v_r.at[home], send_sem=v_ss.at[i], recv_sem=v_rs.at[i],
+            src_ref=values.at[n], dst_ref=values.at[home], send_sem=v_ss.at[i], recv_sem=v_rs.at[i],
             device_id=(w, (n + i) % NARROW), device_id_type=MESH,
         )
 
     def g_copy(q, home):
         chip = (zq // 4 + q // 4) % 4 * 4 + (zq % 4 + q % 4) % 4
         return pltpu.make_async_remote_copy(
-            src_ref=values.at[record], dst_ref=values.at[core * 16 + home],
+            src_ref=values.at[n, core * 16 + zq], dst_ref=values.at[n, core * 16 + home],
             send_sem=g_ss.at[q], recv_sem=g_rs.at[q],
             device_id=(chip * 2 + core, n), device_id_type=MESH,
         )
@@ -177,7 +158,7 @@
     def core_copy(half):
         part = pl.ds(half * 16, 16)
         return pltpu.make_async_remote_copy(
-            src_ref=values.at[part], dst_ref=values.at[part],
+            src_ref=values.at[n, part], dst_ref=values.at[n, part],
             send_sem=core_sem.at[0], recv_sem=core_sem.at[1],
             device_id=(zq * 2 + 1 - core, n), device_id_type=MESH,
         )
@@ -212,13 +193,13 @@
     def compute(to):
         applied = []
         for k in range(CAP):
-            high, low = split(faces[shifted(word[to * CAP + k], 0, 6)])
+            high, low = split(faces[shifted(word[k, to], 0, 6)])
             applied.append(dot(high, p_hi[...]) + dot(low, p_hi[...]) + dot(high, p_lo[...]))
         for k in range(CAP):
             s = to * CAP + k
             high, low = split(applied[k])
             both = dot(pt_hi[...], high) + dot(pt_lo[...], high) + dot(pt_hi[...], low)
-            both = jnp.where(shifted(word[s], 21, 1) > 0, both[0:ROWS, :], 0.0)
+            both = jnp.where(shifted(word[k, to], 21, 1) > 0, both[0:ROWS, :], 0.0)
             edge = both[:, 128:256]
             main_s[s] = both[:, 0:128]
             corner = pltpu.roll(edge[128:ROWS, :], 0, 1, stride=8, stride_axis=0)
@@ -227,11 +208,20 @@
             edge_s[s] = edge
 
     pl.semaphore_wait(barrier, WIDE + NARROW - 2)
-    for i in range(1, NARROW):
-        v_copy(i, n).start()
-    v_r[n] = v_s[...]
+
+    def spread(q, _):
+        g_copy(q, zq).start()
+        return 0
+
+    lax.fori_loop(1, 16, spread, 0)
+    words[...] = jnp.zeros_like(words)
+    for i, row in enumerate(slot_words(elems, slots)):
+        words[i : i + 1, :] = row
+    fetch = pltpu.make_async_copy(words, word, word_sem)
+    fetch.start()
     for i in range(5):
         load(i).wait()
+    fetch.wait()
 
     def send(step, _):
         offset = offset_at(step)
@@ -243,21 +233,7 @@
             main_copy(offset, to, w).start()
             rem_copy(offset, to, w).start()
 
-        @pl.when(step == GATHER_AT)
-        def _():
-            for i in range(1, NARROW):
-                v_copy(i, (n + NARROW - i) % NARROW).wait_recv()
-            for i in range(NARROW):
-                values[record, i] = v_r[i, 0]
-            values[record, NARROW] = v_r[0, 1] + v_r[1, 1] + v_r[2, 1] + v_r[3, 1]
-
-            def spread(q, _):
-                g_copy(q, zq).start()
-                return 0
-
-            lax.fori_loop(1, 16, spread, 0)
-
-        @pl.when(step == SPREAD_AT)
+        @pl.when(step == CORE_AT)
         def _():
             def arrive(q, _):
                 home = (zq // 4 - q // 4 + 4) % 4 * 4 + (zq % 4 - q % 4 + 4) % 4
@@ -266,6 +242,12 @@
 
             lax.fori_loop(1, 16, arrive, 0)
             core_copy(core).start()
+
+        @pl.when(step == NARROW_AT)
+        def _():
+            core_copy(1 - core).wait_recv()
+            for i in range(1, NARROW):
+                v_copy(i, n).start()
 
         return 0
 
@@ -275,18 +257,18 @@
     own_rem = pltpu.make_async_copy(rem_s.at[mine], rem_o.at[mine], own_sem.at[1])
     own_main.start()
     own_rem.start()
-    core_copy(1 - core).wait_recv()
+    for i in range(1, NARROW):
+        v_copy(i, (n + NARROW - i) % NARROW).wait_recv()
 
     def apply(to, _):
         for k in range(CAP):
             s = to * CAP + k
-            row = pl.ds(shifted(word[s], 6, 3), 1)
-            narrow = shifted(word[s], 9, 2)
-            at = shifted(word[s], 11, 1) * 16 + shifted(word[s], 12, 4)
-            head = values[at, narrow, row, :]
-            tail = pltpu.roll(values[at, NARROW, row, :], (128 - 8 * narrow) % 128, 1)
+            row = pl.ds(shifted(word[k, to], 6, 3), 1)
+            narrow = shifted(word[k, to], 9, 2)
+            at = shifted(word[k, to], 11, 1) * 16 + shifted(word[k, to], 12, 4)
+            head, tail = values[narrow, at, 0, row, :], values[narrow, at, 1, row, :]
             y = jnp.sum(main_s[s] * head + edge_s[s] * tail, axis=1, keepdims=True)
-            label = shifted(word[s], 16, 5) * shifted(word[s], 21, 1) - 1 + shifted(word[s], 21, 1)
+            label = shifted(word[k, to], 16, 5) * shifted(word[k, to], 21, 1) - 1 + shifted(word[k, to], 21, 1)
             y = jnp.where(sub == NC, label.astype(jnp.float32), y)
             sums[...] = jnp.where(lane == to * 4 + k, y, sums[...])
         return 0
@@ -375,7 +357,7 @@
     own_rem.wait()
 
 
-def exchange(table, face_blocks, pt, residual, inverse):
+def exchange(elems, slots, face_blocks, pt, residual, inverse):
     hbm = pl.BlockSpec(memory_space=pltpu.HBM)
     vmem = pl.BlockSpec(memory_space=pltpu.VMEM)
     anywhere = pl.BlockSpec(memory_space=pl.ANY)
@@ -387,10 +369,13 @@
             jax.ShapeDtypeStruct((SLOTS, ROWS, 128), f32),
             jax.ShapeDtypeStruct((SLOTS, 8, 128), f32),
         ],
-        in_specs=[hbm] * 5,
+        in_specs=[hbm] * 6,
         out_specs=[vmem, anywhere, anywhere],
         scratch_shapes=[
-            pltpu.SMEM((128,), jnp.int32),
+            pltpu.SMEM((2, FACES), jnp.int32),
+            pltpu.SMEM((WIDE * OWN,), jnp.int32),
+            pltpu.VMEM((8, 128), jnp.int32),
+            pltpu.SMEM((8, 128), jnp.int32),
             pltpu.VMEM((NC, NF), f32),
             pltpu.VMEM((8, NF), f32),
             pltpu.VMEM((NC, 8, NC), f32),
@@ -408,10 +393,9 @@
             pltpu.VMEM((WIDE, 8, 128), f32),
             pltpu.VMEM((NARROW, 16, 128), f32),
             pltpu.VMEM((NARROW, 16, 128), f32),
-            pltpu.VMEM((2, 8, 128), f32),
-            pltpu.VMEM((NARROW, 2, 8, 128), f32),
-            pltpu.VMEM((WIDE, NARROW + 1, 8, 128), f32),
-            dma((4,)),
+            pltpu.VMEM((NARROW, WIDE, 2, 8, 128), f32),
+            dma((5,)),
+            dma(()),
             dma((5,)),
         ]
         + [dma((WIDE,))] * 6
@@ -419,33 +403,48 @@
         + [dma((NARROW,))] * 4
         + [dma((2,))] * 2,
         compiler_params=pltpu.CompilerParams(
-            collective_id=0, has_side_effects=True, vmem_limit_bytes=42 << 20
+            collective_id=0, has_side_effects=True, vmem_limit_bytes=57600 << 10
         ),
         cost_estimate=pl.CostEstimate(flops=10**10, bytes_accessed=35 * 10**6, transcendentals=0),
         name="exchange",
-    )(table, face_blocks, pt, residual, inverse)
-
-
-def unpack_kernel(main, rem, fine_in, out, fine, edge):
+    )(elems, slots, face_blocks, pt, residual, inverse)
+
+
+def unpack_kernel(main_hbm, rem_hbm, fine_in, out, fine, edge, main, rem, sems):
     i = pl.program_id(0)
     rest = NC - 128
 
+    def load(j):
+        part = pl.ds(48 * j, min(48, ROWS - 48 * j))
+        return pltpu.make_async_copy(
+            main_hbm.at[:, part], main.reshape(SLOTS, ROWS, 128).at[:, part], sems.at[j]
+        )
+
+    load_rem = pltpu.make_async_copy(rem_hbm, rem, sems.at[3])
+
     def row(a):
         return main[pl.ds(a, SLOTS, stride=ROWS), :].T
 
     @pl.when(i == 0)
     def _():
+        load(0).start()
+        load_rem.start()
+        load(1).start()
+        load(2).start()
         fine[...] = fine_in[...]
-        for c in range(rest):
-            edge[c] = rem[pl.ds(c, SLOTS, stride=8), :].T
 
     for j in range(NC // PART):
 
         @pl.when(i == j)
         def _(j=j):
+            load(j).wait()
             for r in range(PART):
                 out[r, 0:128, :] = row(j * PART + r)
             size = min(PART, 128 - j * PART)
+            if j == 0:
+                load_rem.wait()
+                for c in range(rest):
+                    edge[c] = rem[pl.ds(c, SLOTS, stride=8), :].T
             for c in range(rest):
                 out[0:size, 128 + c, :] = edge[c, j * PART : j * PART + size, :]
             if size < PART:
@@ -456,6 +455,7 @@
 
 def unpack(main, rem, fine):
     vmem = pl.BlockSpec(memory_space=pltpu.VMEM)
+    hbm = pl.BlockSpec(memory_space=pltpu.HBM)
     return pl.pallas_call(
         unpack_kernel,
         grid=(NC // PART,),
@@ -463,23 +463,27 @@
             jax.ShapeDtypeStruct((NC, NC, SLOTS), jnp.float32),
             jax.ShapeDtypeStruct((8, NF), jnp.float32),
         ],
-        in_specs=[vmem] * 3,
+        in_specs=[hbm, hbm, vmem],
         out_specs=[
             pl.BlockSpec((PART, NC, SLOTS), lambda i: (i, 0, 0)),
             pl.BlockSpec((8, NF), lambda i: (0, 0)),
         ],
-        scratch_shapes=[pltpu.VMEM((NC - 128, 128, SLOTS), jnp.float32)],
-        compiler_params=pltpu.CompilerParams(vmem_limit_bytes=40 << 20),
+        scratch_shapes=[
+            pltpu.VMEM((NC - 128, 128, SLOTS), jnp.float32),
+            pltpu.VMEM((SLOTS * ROWS, 128), jnp.float32),
+            pltpu.VMEM((SLOTS * 8, 128), jnp.float32),
+            pltpu.SemaphoreType.DMA((4,)),
+        ],
+        compiler_params=pltpu.CompilerParams(vmem_limit_bytes=57600 << 10),
         name="unpack",
     )(main, rem, fine)
 
 
 def local(face_blocks, face_elems, coarse_slot, prolong, fine_residual, block_inverse):
-    table = slot_table(face_elems, coarse_slot)
     fine, main, rem = exchange(
-        table, face_blocks, prolong.T, fine_residual, jnp.transpose(block_inverse, (1, 0, 2))
+        face_elems.T, coarse_slot, face_blocks, prolong.T, fine_residual, jnp.transpose(block_inverse, (1, 0, 2))
     )
-    owned, fine = unpack(main.reshape(SLOTS * ROWS, 128), rem.reshape(SLOTS * 8, 128), fine)
+    owned, fine = unpack(main, rem.reshape(SLOTS * 8, 128), fine)
     return fine, jnp.transpose(owned, (2, 0, 1))
 
 

time: 118 us -> 110 us (0.932)
  the two profiles are of different devices: /device:TPU:16 before, /device:TPU:8 now
where the time goes in v4:
time: 110 us; the launch traced here: 109 us
  Pallas kernels  108 us (98%)
    pallas_call x1, Pallas kernels, exchange(): pl.pallas_call(exchange_kernel, out_shape=[jax.ShapeDtypeStruct((8, NF),...  100 us
    pallas_call x1, Pallas kernels, unpack(): pl.pallas_call(unpack_kernel, grid=(NC // PART,), out_shape=[jax.ShapeDty...  7.77 us

profile of v4, /device:TPU:8, one launch (start us, length us, event | category | flops | bytes accessed | tf_op | source)
XLA Modules:
  0.0 108.7 jit_solution(7144774625845257870)
XLA Ops:
  0.6 100.3 %exchange.1 = (f32[8,320]{1,0:T(8,128)}, f32[96,136,128]{2,1,0:T(8,128)}, f32[96,8,128]{2,1,0:T(8,128)}) custom-call(s32[2,40]{1,0:T(2,128)} %bitcast.9, s32[1024]{0:T(1024)} %slots_hbm.1, f32[40,320,320]{2,1,0:T(8,128)} %faces_hbm.1, f32[135,320]{1,0:T(8,128)} %bitcast.8, f32[8,320]{1,0:T(8,128)} %residual_hbm.1, f32[135,8,135]{2,1,0:T(8,128)} %bitcast.7), custom_call_target="tpu_custom_call" | custom-call | flops 10000000000 | bytes 35000000 | tf_op jit(solution)/shard_map/exchange/pallas_call | solution.py:365
  100.9 7.8 %unpack.1 = (f32[135,135,96]{2,1,0:T(8,128)}, f32[8,320]{1,0:T(8,128)}) custom-call(f32[96,136,128]{2,1,0:T(8,128)} %get-tuple-element.7.main_hbm, f32[768,128]{1,0:T(8,128)} %bitcast.5, f32[8,320]{1,0:T(8,128)} %get-tuple-element.9.fine_in), custom_call_target="tpu_custom_call" | custom-call | tf_op jit(solution)/shard_map/unpack/pallas_call | solution.py:459

commit v5 on v4

--- a/solution.py
+++ b/solution.py
@@ -14,7 +14,8 @@
 NF = 320
 NC = 135
 ROWS = 136
-PART = 45
+PART = 27
+CUTS = (0, 32, 56, 88, 112, ROWS)
 FACES = 40
 WIDE = 32
 NARROW = 4
@@ -128,7 +129,14 @@
     for i in range(1, NARROW):
         pl.semaphore_signal(barrier, inc=1, device_id=(w, (n + i) % NARROW), device_id_type=MESH)
 
-    for copy in inputs:
+    for copy in inputs[0:2]:
+        copy.wait()
+    words[...] = jnp.zeros_like(words)
+    for i, row in enumerate(slot_words(elems, slots)):
+        words[i : i + 1, :] = row
+    fetch = pltpu.make_async_copy(words, word, word_sem)
+    fetch.start()
+    for copy in inputs[2:5]:
         copy.wait()
     wide_pt[...] = jnp.zeros_like(wide_pt)
     wide_pt[0:NC, :] = pt[...]
@@ -214,11 +222,6 @@
         return 0
 
     lax.fori_loop(1, 16, spread, 0)
-    words[...] = jnp.zeros_like(words)
-    for i, row in enumerate(slot_words(elems, slots)):
-        words[i : i + 1, :] = row
-    fetch = pltpu.make_async_copy(words, word, word_sem)
-    fetch.start()
     for i in range(5):
         load(i).wait()
     fetch.wait()
@@ -415,12 +418,12 @@
     rest = NC - 128
 
     def load(j):
-        part = pl.ds(48 * j, min(48, ROWS - 48 * j))
+        part = pl.ds(CUTS[j], CUTS[j + 1] - CUTS[j])
         return pltpu.make_async_copy(
             main_hbm.at[:, part], main.reshape(SLOTS, ROWS, 128).at[:, part], sems.at[j]
         )
 
-    load_rem = pltpu.make_async_copy(rem_hbm, rem, sems.at[3])
+    load_rem = pltpu.make_async_copy(rem_hbm, rem, sems.at[5])
 
     def row(a):
         return main[pl.ds(a, SLOTS, stride=ROWS), :].T
@@ -429,8 +432,8 @@
     def _():
         load(0).start()
         load_rem.start()
-        load(1).start()
-        load(2).start()
+        for j in range(1, NC // PART):
+            load(j).start()
         fine[...] = fine_in[...]
 
     for j in range(NC // PART):
@@ -440,7 +443,7 @@
             load(j).wait()
             for r in range(PART):
                 out[r, 0:128, :] = row(j * PART + r)
-            size = min(PART, 128 - j * PART)
+            size = min(PART, 128 - PART * j)
             if j == 0:
                 load_rem.wait()
                 for c in range(rest):
@@ -472,7 +475,7 @@
             pltpu.VMEM((NC - 128, 128, SLOTS), jnp.float32),
             pltpu.VMEM((SLOTS * ROWS, 128), jnp.float32),
             pltpu.VMEM((SLOTS * 8, 128), jnp.float32),
-            pltpu.SemaphoreType.DMA((4,)),
+            pltpu.SemaphoreType.DMA((6,)),
         ],
         compiler_params=pltpu.CompilerParams(vmem_limit_bytes=57600 << 10),
         name="unpack",

time: 110 us -> 110 us (level)
  no operation moved by 1% of the time
where the time goes in v5:
time: 110 us; the launch traced here: 108 us
  Pallas kernels  107 us (97%)
    pallas_call x1, Pallas kernels, exchange(): pl.pallas_call(exchange_kernel, out_shape=[jax.ShapeDtypeStruct((8, NF),...  99.5 us
    pallas_call x1, Pallas kernels, unpack(): pl.pallas_call(unpack_kernel, grid=(NC // PART,), out_shape=[jax.ShapeDty...  7.89 us

profile of v5, /device:TPU:8, one launch (start us, length us, event | category | flops | bytes accessed | tf_op | source)
XLA Modules:
  0.0 108.0 jit_solution(3723513713310453347)
XLA Ops:
  0.6 99.5 %exchange.1 = (f32[8,320]{1,0:T(8,128)}, f32[96,136,128]{2,1,0:T(8,128)}, f32[96,8,128]{2,1,0:T(8,128)}) custom-call(s32[2,40]{1,0:T(2,128)} %bitcast.9, s32[1024]{0:T(1024)} %slots_hbm.1, f32[40,320,320]{2,1,0:T(8,128)} %faces_hbm.1, f32[135,320]{1,0:T(8,128)} %bitcast.8, f32[8,320]{1,0:T(8,128)} %residual_hbm.1, f32[135,8,135]{2,1,0:T(8,128)} %bitcast.7), custom_call_target="tpu_custom_call" | custom-call | flops 10000000000 | bytes 35000000 | tf_op jit(solution)/shard_map/exchange/pallas_call | solution.py:368
  100.1 7.9 %unpack.1 = (f32[135,135,96]{2,1,0:T(8,128)}, f32[8,320]{1,0:T(8,128)}) custom-call(f32[96,136,128]{2,1,0:T(8,128)} %get-tuple-element.7.main_hbm, f32[768,128]{1,0:T(8,128)} %bitcast.5, f32[8,320]{1,0:T(8,128)} %get-tuple-element.9.fine_in), custom_call_target="tpu_custom_call" | custom-call | tf_op jit(solution)/shard_map/unpack/pallas_call | solution.py:462

commit v6 on v5

--- a/solution.py
+++ b/solution.py
@@ -14,8 +14,7 @@
 NF = 320
 NC = 135
 ROWS = 136
-PART = 27
-CUTS = (0, 32, 56, 88, 112, ROWS)
+PART = 45
 FACES = 40
 WIDE = 32
 NARROW = 4
@@ -406,48 +405,33 @@
         + [dma((NARROW,))] * 4
         + [dma((2,))] * 2,
         compiler_params=pltpu.CompilerParams(
-            collective_id=0, has_side_effects=True, vmem_limit_bytes=57600 << 10
+            collective_id=0, has_side_effects=True, vmem_limit_bytes=42 << 20
         ),
         cost_estimate=pl.CostEstimate(flops=10**10, bytes_accessed=35 * 10**6, transcendentals=0),
         name="exchange",
     )(elems, slots, face_blocks, pt, residual, inverse)
 
 
-def unpack_kernel(main_hbm, rem_hbm, fine_in, out, fine, edge, main, rem, sems):
+def unpack_kernel(main, rem, fine_in, out, fine, edge):
     i = pl.program_id(0)
     rest = NC - 128
 
-    def load(j):
-        part = pl.ds(CUTS[j], CUTS[j + 1] - CUTS[j])
-        return pltpu.make_async_copy(
-            main_hbm.at[:, part], main.reshape(SLOTS, ROWS, 128).at[:, part], sems.at[j]
-        )
-
-    load_rem = pltpu.make_async_copy(rem_hbm, rem, sems.at[5])
-
     def row(a):
         return main[pl.ds(a, SLOTS, stride=ROWS), :].T
 
     @pl.when(i == 0)
     def _():
-        load(0).start()
-        load_rem.start()
-        for j in range(1, NC // PART):
-            load(j).start()
         fine[...] = fine_in[...]
+        for c in range(rest):
+            edge[c] = rem[pl.ds(c, SLOTS, stride=8), :].T
 
     for j in range(NC // PART):
 
         @pl.when(i == j)
         def _(j=j):
-            load(j).wait()
             for r in range(PART):
                 out[r, 0:128, :] = row(j * PART + r)
-            size = min(PART, 128 - PART * j)
-            if j == 0:
-                load_rem.wait()
-                for c in range(rest):
-                    edge[c] = rem[pl.ds(c, SLOTS, stride=8), :].T
+            size = min(PART, 128 - j * PART)
             for c in range(rest):
                 out[0:size, 128 + c, :] = edge[c, j * PART : j * PART + size, :]
             if size < PART:
@@ -458,7 +442,6 @@
 
 def unpack(main, rem, fine):
     vmem = pl.BlockSpec(memory_space=pltpu.VMEM)
-    hbm = pl.BlockSpec(memory_space=pltpu.HBM)
     return pl.pallas_call(
         unpack_kernel,
         grid=(NC // PART,),
@@ -466,27 +449,23 @@
             jax.ShapeDtypeStruct((NC, NC, SLOTS), jnp.float32),
             jax.ShapeDtypeStruct((8, NF), jnp.float32),
         ],
-        in_specs=[hbm, hbm, vmem],
+        in_specs=[vmem] * 3,
         out_specs=[
             pl.BlockSpec((PART, NC, SLOTS), lambda i: (i, 0, 0)),
             pl.BlockSpec((8, NF), lambda i: (0, 0)),
         ],
-        scratch_shapes=[
-            pltpu.VMEM((NC - 128, 128, SLOTS), jnp.float32),
-            pltpu.VMEM((SLOTS * ROWS, 128), jnp.float32),
-            pltpu.VMEM((SLOTS * 8, 128), jnp.float32),
-            pltpu.SemaphoreType.DMA((6,)),
-        ],
-        compiler_params=pltpu.CompilerParams(vmem_limit_bytes=57600 << 10),
+        scratch_shapes=[pltpu.VMEM((NC - 128, 128, SLOTS), jnp.float32)],
+        compiler_params=pltpu.CompilerParams(vmem_limit_bytes=40 << 20),
         name="unpack",
     )(main, rem, fine)
 
 
 def local(face_blocks, face_elems, coarse_slot, prolong, fine_residual, block_inverse):
-    fine, main, rem = exchange(
+    inputs = (
         face_elems.T, coarse_slot, face_blocks, prolong.T, fine_residual, jnp.transpose(block_inverse, (1, 0, 2))
     )
-    owned, fine = unpack(main, rem.reshape(SLOTS * 8, 128), fine)
+    fine, main, rem = exchange(*(pltpu.with_memory_space_constraint(x, pltpu.HBM) for x in inputs))
+    owned, fine = unpack(main.reshape(SLOTS * ROWS, 128), rem.reshape(SLOTS * 8, 128), fine)
     return fine, jnp.transpose(owned, (2, 0, 1))
 
 

time: 110 us -> 106 us (0.964)
  Pallas kernels: 107 us -> 104 us
    pallas_call x1, Pallas kernels: 7.89 us -> 5.21 us  [unpack(): pl.pallas_call(unpack_kernel, grid=(NC // PART,), out_shape=[jax.ShapeDty...]
where the time goes in v6:
time: 106 us; the launch traced here: 105 us
  Pallas kernels  104 us (98%)
    pallas_call x1, Pallas kernels, exchange(): pl.pallas_call(exchange_kernel, out_shape=[jax.ShapeDtypeStruct((8, NF),...  98.7 us
    pallas_call x1, Pallas kernels, unpack(): pl.pallas_call(unpack_kernel, grid=(NC // PART,), out_shape=[jax.ShapeDty...  5.21 us

profile of v6, /device:TPU:8, one launch (start us, length us, event | category | flops | bytes accessed | tf_op | source)
XLA Modules:
  0.0 104.6 jit_solution(7510269671028748845)
XLA Ops:
  0.6 98.7 %exchange.1 = (f32[8,320]{1,0:T(8,128)S(1)}, f32[96,136,128]{2,1,0:T(8,128)S(1)}, f32[96,8,128]{2,1,0:T(8,128)S(1)}) custom-call(s32[2,40]{1,0:T(2,128)} %bitcast.11, s32[1024]{0:T(1024)} %slots_hbm.1, f32[40,320,320]{2,1,0:T(8,128)} %faces_hbm.1, f32[135,320]{1,0:T(8,128)} %bitcast.10, f32[8,320]{1,0:T(8,128)} %residual_hbm.1, f32[135,8,135]{2,1,0:T(8,128)} %bitcast.9), custom_call_target="tpu_custom_call" | custom-call | flops 10000000000 | bytes 35000000 | tf_op jit(solution)/shard_map/exchange/pallas_call | solution.py:367
  99.4 5.2 %unpack.1 = (f32[135,135,96]{2,1,0:T(8,128)}, f32[8,320]{1,0:T(8,128)}) custom-call(f32[13056,128]{1,0:T(8,128)S(1)} %bitcast.6, f32[768,128]{1,0:T(8,128)S(1)} %bitcast.7, f32[8,320]{1,0:T(8,128)S(1)} %get-tuple-element.9.fine_in), custom_call_target="tpu_custom_call" | custom-call | tf_op jit(solution)/shard_map/unpack/pallas_call | solution.py:445

commit v7 on v6

--- a/solution.py
+++ b/solution.py
@@ -99,7 +99,7 @@
     n = lax.axis_index("narrow")
 
     def load(i):
-        part = pl.ds(i * 8, 8)
+        part = pl.ds(i * 5, 5)
         return pltpu.make_async_copy(faces_hbm.at[part], faces.at[part], face_sem.at[i])
 
     inputs = [
@@ -110,7 +110,7 @@
     ]
     for copy in inputs:
         copy.start()
-    for i in range(5):
+    for i in range(8):
         load(i).start()
 
     def partner(offset, sign):
@@ -221,7 +221,7 @@
         return 0
 
     lax.fori_loop(1, 16, spread, 0)
-    for i in range(5):
+    for i in range(8):
         load(i).wait()
     fetch.wait()
 
@@ -398,7 +398,7 @@
             pltpu.VMEM((NARROW, WIDE, 2, 8, 128), f32),
             dma((5,)),
             dma(()),
-            dma((5,)),
+            dma((8,)),
         ]
         + [dma((WIDE,))] * 6
         + [dma((16,))] * 2

time: 106 us -> 107 us (level)
  no operation moved by 1% of the time
where the time goes in v7:
time: 107 us; the launch traced here: 105 us
  Pallas kernels  104 us (97%)
    pallas_call x1, Pallas kernels, exchange(): pl.pallas_call(exchange_kernel, out_shape=[jax.ShapeDtypeStruct((8, NF),...  99.2 us
    pallas_call x1, Pallas kernels, unpack(): pl.pallas_call(unpack_kernel, grid=(NC // PART,), out_shape=[jax.ShapeDty...  5.21 us

profile of v7, /device:TPU:8, one launch (start us, length us, event | category | flops | bytes accessed | tf_op | source)
XLA Modules:
  0.0 105.0 jit_solution(36235017949719876)
XLA Ops:
  0.6 99.2 %exchange.1 = (f32[8,320]{1,0:T(8,128)S(1)}, f32[96,136,128]{2,1,0:T(8,128)S(1)}, f32[96,8,128]{2,1,0:T(8,128)S(1)}) custom-call(s32[2,40]{1,0:T(2,128)} %bitcast.11, s32[1024]{0:T(1024)} %slots_hbm.1, f32[40,320,320]{2,1,0:T(8,128)} %faces_hbm.1, f32[135,320]{1,0:T(8,128)} %bitcast.10, f32[8,320]{1,0:T(8,128)} %residual_hbm.1, f32[135,8,135]{2,1,0:T(8,128)} %bitcast.9), custom_call_target="tpu_custom_call" | custom-call | flops 10000000000 | bytes 35000000 | tf_op jit(solution)/shard_map/exchange/pallas_call | solution.py:367
  99.8 5.2 %unpack.1 = (f32[135,135,96]{2,1,0:T(8,128)}, f32[8,320]{1,0:T(8,128)}) custom-call(f32[13056,128]{1,0:T(8,128)S(1)} %bitcast.6, f32[768,128]{1,0:T(8,128)S(1)} %bitcast.7, f32[8,320]{1,0:T(8,128)S(1)} %get-tuple-element.9.fine_in), custom_call_target="tpu_custom_call" | custom-call | tf_op jit(solution)/shard_map/unpack/pallas_call | solution.py:445
